TPU v7x, 256 devices: a whole 4x4x8 slice. The times are simulated.
256 devices in a mesh: snap: 64 (over z_hi, y, x, core), row: 4 (over z_lo).
Axes of the slice: x: 4, y: 4, z: 8 (z_hi: 2, z_lo: 4; z = z_hi * 4 + z_lo), core: 2. Of those that a mesh axis runs over, the one named last changes fastest.
Arguments:
- delay_matrix: float32 [128, 32, 16384], P('snap', 'row'), may hold values from -6 to 6
- arrangement: int32 [128], replicated, may hold values from 0 to 127, each once
- rotations: float32 [2, 64, 256, 256], P(None, 'snap'), may hold values from -1 to 2
Outputs:
- rotated: float32 [128, 32, 16384], P(None, 'row', 'snap')
- pair_grams: float32 [2, 64, 256, 256], P(None, 'snap', 'row')
Inputs may be any that keep to these rules, and one draw needn't show every extreme that they name: arrangement names every block once.
All inputs are finite; a program needn't handle non-finite values.
Results may differ from a plain program's by a relative error of at most 0.00007.
Values sent between devices are 32-bit elements; how exact they have to be, the bound alone decides.
A program may use at most 128 MiB of HBM per device.

v0:
```python
import jax
import jax.numpy as jnp
from jax import lax
from jax.sharding import PartitionSpec as P

MODES = 128
DELAYS = 32


highest = lax.Precision.HIGHEST


def product(left_part, right_part):
    return jnp.dot(left_part, right_part, precision=highest, preferred_element_type=jnp.float32)


def inner_product(left_part, right_part):
    return lax.dot_general(
        left_part,
        right_part,
        (((0,), (0,)), ((), ())),
        precision=highest,
        preferred_element_type=jnp.float32,
    )


def body(delay_matrix, arrangement, rotations):
    mode_part, delay_part, column_count = delay_matrix.shape
    pair_count = lax.axis_size("snap")
    block_width = column_count // (2 * pair_count)
    share_rows = 2 * block_width // lax.axis_size("row")
    row_index = lax.axis_index("row")
    row_scale = float(MODES * DELAYS)

    def turn_pair(paired, rotation):
        matrix = paired.reshape(-1, 2 * block_width)
        turned_matrix = product(matrix, rotation)
        turned = turned_matrix.reshape(paired.shape)
        gram_part = lax.psum(inner_product(matrix, matrix), "row") / row_scale
        left_part = lax.dynamic_slice_in_dim(rotation, row_index * share_rows, share_rows, 1)
        pair_gram = product(inner_product(left_part, gram_part), rotation)
        return (turned, pair_gram)

    local_blocks = delay_matrix.reshape(mode_part, delay_part, 2 * pair_count, block_width)
    placed = jnp.take(local_blocks, arrangement, axis=2).reshape(
        mode_part, delay_part, column_count
    )
    paired_one = lax.all_to_all(placed, "snap", split_axis=2, concat_axis=0, tiled=True)
    turned_one, gram_one = turn_pair(paired_one, rotations[0, 0])
    row_layout = lax.all_to_all(turned_one, "snap", split_axis=0, concat_axis=2, tiled=True)
    viewed = row_layout.reshape(mode_part, delay_part, pair_count, 2, block_width)
    reordered = jnp.stack([viewed[:, :, :, 0], jnp.roll(viewed[:, :, :, 1], 1, axis=2)], axis=3)
    reordered = reordered.reshape(mode_part, delay_part, column_count)
    paired_two = lax.all_to_all(reordered, "snap", split_axis=2, concat_axis=0, tiled=True)
    turned_two, gram_two = turn_pair(paired_two, rotations[1, 0])
    return (turned_two, jnp.stack([gram_one, gram_two])[:, None])


def solution(mesh):
    placed = (P("snap", "row", None), P(), P(None, "snap", None, None))
    return jax.shard_map(
        body,
        mesh=mesh,
        in_specs=placed,
        out_specs=(P(None, "row", "snap"), P(None, "snap", "row", None)),
        check_vma=False,
    )
```

profile of v0, /device:TPU:224, one launch (start us, length us, event | category | flops | bytes accessed | tf_op | source)
XLA Modules:
  0.0 363.9 jit_solution(13275988195117088096)
XLA Ops:
  9.5 14.7 %copy.22 = f32[2,8,16384]{1,0,2:T(2,128)} copy(f32[2,8,16384]{2,1,0:T(8,128)S(1)} %bitcast_select_fusion) | data formatting | bytes 2097152 | tf_op jit(solution)/shard_map/jit(_take)/select_n | solution.py:45
  24.2 28.3 %reshape.50 = f32[64,1,4096]{2,1,0:T(1,128)S(1)} reshape(f32[16384,2,8]{2,1,0:T(2,128)} %bitcast.84) | data formatting | bytes 2097152
  52.5 30.3 %all_to_all.45 = f32[64,1,4096]{2,1,0:T(1,128)S(1)} all-to-all(f32[64,1,4096]{2,1,0:T(1,128)S(1)} %reshape.50), channel_id=1, replica_groups=mesh['snap'=64,'row'=4] {'snap'}, dimensions={0} | all-to-all | bytes 2097152 | tf_op jit(solution)/shard_map/all_to_all | solution.py:48
  83.3 3.3 reduce
  86.6 26.7 %reshape.51 = f32[16384,2,8]{2,1,0:T(2,128)} reshape(f32[64,4096]{1,0:T(8,128)S(1)} %reduce) | data formatting | bytes 2097152
  113.3 17.6 %copy.48 = f32[2,8,64,256]{3,1,0,2:T(8,128)S(1)} copy(f32[2,8,64,256]{1,0,3,2:T(2,128)} %bitcast.80) | data formatting | bytes 2097152 | tf_op jit(solution)/shard_map/all_to_all | solution.py:48
  130.9 1.0 fusion.4
  131.9 40.9 %all_to_all.46 = f32[128,8,256]{2,1,0:T(8,128)S(1)} all-to-all(f32[128,8,256]{2,1,0:T(8,128)S(1)} %fusion.4), channel_id=1, replica_groups=mesh['snap'=64,'row'=4] {'snap'}, dimensions={0} | all-to-all | bytes 2097152 | tf_op jit(solution)/shard_map/all_to_all | solution.py:50
  174.0 1.1 fusion.26
  175.3 11.2 %copy.42 = f32[2,8,64,2,128]{1,0,4,3,2:T(2,128)} copy(f32[2,8,64,2,128]{4,2,1,0,3:T(8,128)S(1)} %pad_maximum_fusion) | data formatting | bytes 2097152 | tf_op jit(solution)/shard_map/reshape | solution.py:53
  186.5 29.0 %reshape.52 = f32[64,1,4096]{2,1,0:T(1,128)} reshape(f32[16384,2,8]{2,1,0:T(2,128)} %bitcast.85) | data formatting | bytes 2097152
  215.4 13.8 %all-to-all-start.2 = ((f32[64,1,4096]{2,1,0:T(1,128)}), f32[64,1,4096]{2,1,0:T(1,128)S(1)}, u32[]{:S(2)}, u32[]{:S(2)}) async-start(f32[64,1,4096]{2,1,0:T(1,128)} %reshape.52), calls=%async_computation.2 | async-start | bytes 2097152 | tf_op jit(solution)/shard_map/all_to_all | solution.py:54
  229.3 13.2 %copy.40 = f32[2,8,64,256]{3,2,1,0:T(8,128)S(1)} copy(f32[2,8,64,256]{1,0,3,2:T(2,128)} %bitcast.81) | data formatting | bytes 2097152 | tf_op jit(solution)/shard_map/all_to_all | solution.py:48
  242.5 2.5 convolution_bitcast_fusion.1
  245.0 7.1 %all-to-all-done.2 = f32[64,1,4096]{2,1,0:T(1,128)S(1)} async-done(((f32[64,1,4096]{2,1,0:T(1,128)}), f32[64,1,4096]{2,1,0:T(1,128)S(1)}, u32[]{:S(2)}, u32[]{:S(2)}) %all-to-all-start.2) | async-done | bytes 1048608 | tf_op jit(solution)/shard_map/all_to_all | solution.py:54
  252.1 3.3 reduce.1
  255.4 26.7 %reshape.53 = f32[16384,2,8]{2,1,0:T(2,128)} reshape(f32[64,4096]{1,0:T(8,128)S(1)} %reduce.1) | data formatting | bytes 2097152
  282.1 13.2 %copy.43 = f32[2,8,64,256]{3,2,1,0:T(8,128)S(1)} copy(f32[2,8,64,256]{1,0,3,2:T(2,128)} %bitcast.82) | data formatting | bytes 2097152 | tf_op jit(solution)/shard_map/all_to_all | solution.py:54
  295.3 2.5 convolution_bitcast_fusion
  298.0 17.6 %copy.49 = f32[2,8,64,256]{3,1,0,2:T(8,128)S(1)} copy(f32[2,8,64,256]{1,0,3,2:T(2,128)} %bitcast.83) | data formatting | bytes 2097152 | tf_op jit(solution)/shard_map/all_to_all | solution.py:54
  315.6 2.0 fusion.2
  317.6 35.5 %all-reduce.3.cloned.1.call-done = (f32[256,256]{1,0:T(8,128)}, f32[256,256]{1,0:T(8,128)}) async-done(((f32[256,256]{1,0:T(8,128)}, f32[256,256]{1,0:T(8,128)}), (f32[256,256]{1,0:T(8,128)}, f32[256,256]{1,0:T(8,128)})) %all-reduce.3.cloned.1.call-update) | async-done | bytes 524304 | tf_op jit(solution)/shard_map/psum | solution.py:39
  353.1 1.4 fusion.8
  354.8 1.4 fusion.10
  (24 shorter events, 5.4 us)
Async XLA Ops:
  7.2 1.5 copy-start
  86.6 44.3 %copy-start.2 = (f32[2,1,256,256]{3,2,1,0:T(8,128)S(1)}, f32[2,1,256,256]{3,2,1,0:T(8,128)}, u32[]{:S(2)}) copy-start(f32[2,1,256,256]{3,2,1,0:T(8,128)} %param.5) | copy-start | bytes 1572868
  215.4 36.7 %all-to-all-start.2 = ((f32[64,1,4096]{2,1,0:T(1,128)}), f32[64,1,4096]{2,1,0:T(1,128)S(1)}, u32[]{:S(2)}, u32[]{:S(2)}) async-start(f32[64,1,4096]{2,1,0:T(1,128)} %reshape.52), calls=%async_computation.2 | async-start | bytes 2097152 | tf_op jit(solution)/shard_map/all_to_all | solution.py:54
  229.2 123.9 %all-reduce.3.cloned.1.call-start = ((), (), s32[]{:S(2)}) async-start(), calls=%async_computation.3 | async-start | bytes 1048576 | tf_op jit(solution)/shard_map/psum | solution.py:39
  282.1 75.0 %copy-start.1 = (f32[2,8,16384]{2,1,0:T(8,128)S(1)}, f32[2,8,16384]{2,1,0:T(8,128)}, u32[]{:S(2)}) copy-start(f32[2,8,16384]{2,1,0:T(8,128)} %param.3) | copy-start | bytes 3145732
Sparse Core Ops, SparseCore 0:
  298.0 55.0 all-reduce.2
where the time goes:
time: 369 us; the launch traced here: 364 us
  local copies, waits for them, and re-layouts  202 us (55%)
  blocking collectives  71.2 us (19%)
  waiting for transfers between devices  42.7 us (12%)
  between operations  14.2 us (4%)
  starting transfers between devices  13.9 us (4%)
  matrix products  11.3 us (3%)
  other arithmetic  8.84 us (2%)
    unnamed x10, local copies, waits for them, and re-layouts  111 us
    all_to_all x1, blocking collectives, body(): lax.all_to_all(turned_one, 'snap', split_axis=0, concat_axis=2, tiled=True)  40.9 us
    psum x1, waiting for transfers between devices, turn_pair(): gram_part = lax.psum(inner_product(matrix, matrix), 'row') / row_scale  35.5 us
    all_to_all x3, local copies, waits for them, and re-layouts, body(): lax.all_to_all(placed, 'snap', split_axis=2, concat_axis=0, tiled=True)  31.3 us
    all_to_all x2, local copies, waits for them, and re-layouts, body(): lax.all_to_all(reordered, 'snap', split_axis=2, concat_axis=0, tiled=True)  30.9 us
    all_to_all x1, blocking collectives, body(): lax.all_to_all(placed, 'snap', split_axis=2, concat_axis=0, tiled=True)  30.3 us
    select_n x1, local copies, waits for them, and re-layouts, body(): jnp.take(local_blocks, arrangement, axis=2)  14.7 us
    all_to_all x1, starting transfers between devices, body(): lax.all_to_all(reordered, 'snap', split_axis=2, concat_axis=0, tiled=True)  13.8 us
  transfers between devices with their start and end apart: 2, of which 2 were waited for; matrix products, arithmetic and copies ran while one was open for 10% of the time, Pallas kernels for 0%

commit v1 on v0

v1 whole, which is shorter than its diff:
```python
import functools

import jax
import jax.numpy as jnp
from jax import lax
from jax.experimental import pallas as pl
from jax.experimental.pallas import tpu as pltpu
from jax.sharding import PartitionSpec as P

MESH = pl.DeviceIdType.MESH
GROUPS = 8


def split(value):
    high = value.astype(jnp.bfloat16)
    low = (value - high.astype(jnp.float32)).astype(jnp.bfloat16)
    return high, low


def dot(left, right):
    return jnp.dot(left, right, preferred_element_type=jnp.float32)


def dot_rows(left, right):
    return lax.dot_general(left, right, (((0,), (0,)), ((), ())), preferred_element_type=jnp.float32)


def kernel(
    sizes,
    order_ref,
    x_ref,
    rot_ref,
    out_ref,
    gram_ref,
    stage,
    blocks,
    first,
    second,
    arrived,
    result,
    rot_high,
    rot_low,
    sums,
    shares,
    share_in,
    a2a_send,
    a2a_recv,
    next_send,
    next_recv,
    out_sem,
    share_send,
    share_recv,
):
    snaps, rows, modes, delays, width = sizes
    half = width // 2
    per_group = snaps // GROUPS
    group_modes = modes * per_group
    group_rows = group_modes * delays
    share_rows = width // rows
    scale = 1.0 / float(modes * snaps * delays * rows)

    me = lax.axis_index("snap")
    row = lax.axis_index("row")
    my_group = me // per_group
    after = (me + 1) % snaps

    barrier = pltpu.get_barrier_semaphore()

    @pl.loop(1, snaps)
    def _(i):
        pl.semaphore_signal(
            barrier, inc=1, device_id={"snap": (me + i) % snaps, "row": row}, device_id_type=MESH
        )

    for i in range(1, rows):
        pl.semaphore_signal(
            barrier, inc=1, device_id={"snap": me, "row": (row + i) % rows}, device_id_type=MESH
        )

    @pl.loop(0, snaps, unroll=4)
    def _(d):
        stage[d, :, :, :half] = x_ref[:, order_ref[2 * d]]
        stage[d, :, :, half:] = x_ref[:, order_ref[2 * d + 1]]

    for r in range(2):
        high, low = split(rot_ref[r, 0])
        rot_high[r] = high
        rot_low[r] = low
    sums[...] = jnp.zeros_like(sums)
    blocks[pl.ds(me * modes, modes)] = stage[me]

    pl.semaphore_wait(barrier, snaps - 1 + rows - 1)

    def send_blocks(d):
        pltpu.make_async_remote_copy(
            src_ref=stage.at[d],
            dst_ref=blocks.at[pl.ds(me * modes, modes)],
            send_sem=a2a_send,
            recv_sem=a2a_recv.at[my_group],
            device_id={"snap": d, "row": row},
            device_id_type=MESH,
        ).start()

    low_part = me % (snaps // 2)
    high_part = me // (snaps // 2)
    ys = GROUPS // 2
    my_y = my_group % ys
    my_place = me % per_group

    @pl.loop(0, ys)
    def _(k):
        @pl.loop(0, per_group)
        def _(j):
            place = ((my_y + k) % ys) * per_group + (my_place + j) % per_group
            send_blocks((1 - high_part) * (snaps // 2) + place)

            @pl.when(k + j > 0)
            def _():
                send_blocks(high_part * (snaps // 2) + place)

    def wait_group(group):
        whole = blocks.at[pl.ds(0, group_modes)]
        part = blocks.at[pl.ds(0, group_modes - modes)]

        @pl.when(group == my_group)
        def _():
            pltpu.make_async_copy(part, part, a2a_recv.at[group]).wait()

        @pl.when(group != my_group)
        def _():
            pltpu.make_async_copy(whole, whole, a2a_recv.at[group]).wait()

    def turn(r, matrix):
        high, low = split(matrix)
        turned = dot(high, rot_high[r]) + (dot(high, rot_low[r]) + dot(low, rot_high[r]))
        high, low = split(turned)
        sums[r, :, :width] += dot_rows(high, high)
        sums[r, :, width:] += dot_rows(high, low)
        return turned

    def send_next(group):
        span = pl.ds(group * group_modes, group_modes)
        return pltpu.make_async_remote_copy(
            src_ref=second.at[span],
            dst_ref=arrived.at[span],
            send_sem=next_send,
            recv_sem=next_recv.at[group],
            device_id={"snap": after, "row": row},
            device_id_type=MESH,
        )

    def group_at(k, turned_by):
        part = (high_part + k // ys) % 2
        return part * ys + (my_y + ys - (k + turned_by) % ys) % ys

    def round_one(k):
        group = group_at(k, 0)
        span = pl.ds(group * group_modes, group_modes)
        wait_group(group)
        turned = turn(0, blocks[span].reshape(group_rows, width))
        turned = turned.reshape(group_modes, delays, width)
        first[span] = turned[:, :, :half]
        second[span] = turned[:, :, half:]
        send_next(group).start()

    wraps = jnp.where(my_place == 0, 1, 0)

    def round_two(k):
        group = group_at(k, wraps)
        span = pl.ds(group * group_modes, group_modes)
        send_next(group).wait_recv()
        matrix = jnp.concatenate([first[span], arrived[span]], axis=2)
        turned = turn(1, matrix.reshape(group_rows, width))
        result[span] = turned.reshape(group_modes, delays, width)
        pltpu.make_async_copy(result.at[span], out_ref.at[span], out_sem).start()

    def finish(r):
        cross = sums[r, :, width:]
        total = (sums[r, :, :width] + (cross + cross.T)) * scale
        shares[r] = total.reshape(rows, share_rows, width)
        for i in range(1, rows):
            share_copy(r, i).start()

    def share_copy(r, i):
        to = (row + i) % rows
        return pltpu.make_async_remote_copy(
            src_ref=shares.at[r, to],
            dst_ref=share_in.at[r, i],
            send_sem=share_send.at[r, i],
            recv_sem=share_recv.at[r, i],
            device_id={"snap": me, "row": to},
            device_id_type=MESH,
        )

    def collect(r):
        for i in range(1, rows):
            share_copy(r, i).wait()
        total = shares[r, row]
        for i in range(1, rows):
            total = total + share_in[r, i]
        gram_ref[r, 0] = total

    round_one(0)

    @pl.loop(1, GROUPS)
    def _(k):
        round_one(k)
        round_two(k - 1)

    finish(0)
    round_two(GROUPS - 1)
    finish(1)
    collect(0)
    everything = stage.at[pl.ds(0, snaps - 1)]
    pltpu.make_async_copy(everything, everything, a2a_send).wait()
    pltpu.make_async_copy(second, second, next_send).wait()
    pltpu.make_async_copy(result, out_ref, out_sem).wait()
    collect(1)


def body(delay_matrix, arrangement, rotations):
    modes, delays, columns = delay_matrix.shape
    snaps = lax.axis_size("snap")
    rows = lax.axis_size("row")
    width = columns // snaps
    half = width // 2
    share_rows = width // rows
    sizes = (snaps, rows, modes, delays, width)
    f32, bf16 = jnp.float32, jnp.bfloat16
    blocks = delay_matrix.reshape(modes, delays, 2 * snaps, half).transpose(0, 2, 1, 3)
    vmem = pl.BlockSpec(memory_space=pltpu.VMEM)
    return pl.pallas_call(
        functools.partial(kernel, sizes),
        out_shape=(
            jax.ShapeDtypeStruct((snaps * modes, delays, width), f32),
            jax.ShapeDtypeStruct((2, 1, share_rows, width), f32),
        ),
        in_specs=[pl.BlockSpec(memory_space=pltpu.SMEM), vmem, vmem],
        out_specs=(pl.BlockSpec(memory_space=pl.ANY), vmem),
        scratch_shapes=[
            pltpu.VMEM((snaps, modes, delays, width), f32),
            pltpu.VMEM((snaps * modes, delays, width), f32),
            pltpu.VMEM((snaps * modes, delays, half), f32),
            pltpu.VMEM((snaps * modes, delays, half), f32),
            pltpu.VMEM((snaps * modes, delays, half), f32),
            pltpu.VMEM((snaps * modes, delays, width), f32),
            pltpu.VMEM((2, width, width), bf16),
            pltpu.VMEM((2, width, width), bf16),
            pltpu.VMEM((2, width, 2 * width), f32),
            pltpu.VMEM((2, rows, share_rows, width), f32),
            pltpu.VMEM((2, rows, share_rows, width), f32),
            pltpu.SemaphoreType.DMA,
            pltpu.SemaphoreType.DMA((GROUPS,)),
            pltpu.SemaphoreType.DMA,
            pltpu.SemaphoreType.DMA((GROUPS,)),
            pltpu.SemaphoreType.DMA,
            pltpu.SemaphoreType.DMA((2, rows)),
            pltpu.SemaphoreType.DMA((2, rows)),
        ],
        compiler_params=pltpu.CompilerParams(
            collective_id=0, has_side_effects=True, vmem_limit_bytes=32 * 1024 * 1024
        ),
        name="rounds",
    )(arrangement, blocks, rotations)


def solution(mesh):
    placed = (P("snap", "row", None), P(), P(None, "snap", None, None))
    return jax.shard_map(
        body,
        mesh=mesh,
        in_specs=placed,
        out_specs=(P(None, "row", "snap"), P(None, "snap", "row", None)),
        check_vma=False,
    )
```

time: 369 us -> 75.8 us (0.21); the launches traced: 364 us -> 75.4 us
  local copies, waits for them, and re-layouts: 202 us -> 4.54 us
  blocking collectives: 71.2 us -> 0 us
  Pallas kernels: 0 us -> 70.2 us
  waiting for transfers between devices: 42.7 us -> 0 us
  starting transfers between devices: 13.9 us -> 0 us
  between operations: 14.2 us -> 0.65 us
  matrix products: 11.3 us -> 0 us
  other arithmetic: 8.84 us -> 0 us
    unnamed x10 -> x8, local copies, waits for them, and re-layouts: 111 us -> 4.54 us
    all_to_all x2 -> x0, blocking collectives: 71.2 us -> none  [the longest x1 40.9 us: body(): lax.all_to_all(turned_one, 'snap', split_axis=0, concat_axis=2, tiled=True)]
    pallas_call x0 -> x1, Pallas kernels: none -> 70.2 us  [body(): pl.pallas_call(functools.partial(kernel, sizes), out_shape=(jax.ShapeDtyp...]
    all_to_all x6 -> x0, local copies, waits for them, and re-layouts: 62.8 us -> none  [the longest x3 31.3 us: body(): lax.all_to_all(placed, 'snap', split_axis=2, concat_axis=0, tiled=True)]
    psum x1 -> x0, waiting for transfers between devices: 35.5 us -> none  [turn_pair(): gram_part = lax.psum(inner_product(matrix, matrix), 'row') / row_scale]
    select_n x1 -> x0, local copies, waits for them, and re-layouts: 14.7 us -> none  [body(): jnp.take(local_blocks, arrangement, axis=2)]
    all_to_all x1 -> x0, starting transfers between devices: 13.8 us -> none  [body(): lax.all_to_all(reordered, 'snap', split_axis=2, concat_axis=0, tiled=True)]
    reshape x2 -> x0, local copies, waits for them, and re-layouts: 11.7 us -> none  [the longest x1 11.2 us: body(): reordered = reordered.reshape(mode_part, delay_part, column_count)]
  transfers between devices with their start and end apart: 2 -> 0, of which waited for: 2 -> 0; matrix products, arithmetic and copies ran while one was open for 10% -> 0% of each run, Pallas kernels for 0% -> 0%
where the time goes in v1:
time: 75.8 us; the launch traced here: 75.4 us
  Pallas kernels  70.2 us (93%)
  local copies, waits for them, and re-layouts  4.54 us (6%)
    pallas_call x1, Pallas kernels, body(): pl.pallas_call(functools.partial(kernel, sizes), out_shape=(jax.ShapeDtyp...  70.2 us
    unnamed x8, local copies, waits for them, and re-layouts  4.54 us

profile of v1, /device:TPU:224, one launch (start us, length us, event | category | flops | bytes accessed | tf_op | source)
XLA Modules:
  0.0 75.4 jit_solution(4823782708707323904)
XLA Ops:
  0.6 0.0 copy-start.2
  0.6 0.6 copy-done.2
  1.3 0.0 copy-start
  1.3 1.2 %copy-done = f32[2,8,16384]{2,1,0:T(8,128)S(1)} copy-done((f32[2,8,16384]{2,1,0:T(8,128)S(1)}, f32[2,8,16384]{2,1,0:T(8,128)}, u32[]{:S(2)}) %copy-start) | copy-done | bytes 1048600
  2.5 0.0 copy-start.1
  2.5 1.0 %copy-done.1 = f32[2,1,256,256]{3,2,1,0:T(8,128)S(1)} copy-done((f32[2,1,256,256]{3,2,1,0:T(8,128)S(1)}, f32[2,1,256,256]{3,2,1,0:T(8,128)}, u32[]{:S(2)}) %copy-start.1) | copy-done | bytes 524312
  3.6 70.2 %rounds.1 = (f32[128,8,256]{2,1,0:T(8,128)S(1)}, f32[2,1,64,256]{3,2,1,0:T(8,128)S(1)}) custom-call(s32[128]{0:T(128)S(1)} %copy-done.2, f32[2,128,8,128]{3,2,1,0:T(8,128)S(1)} %bitcast.3, f32[2,1,256,256]{3,2,1,0:T(8,128)S(1)} %copy-done.1), custom_call_target="tpu_custom_call" | custom-call | tf_op jit(solution)/shard_map/rounds/pallas_call | solution.py:232
  73.8 1.0 %copy.7 = f32[128,8,256]{2,1,0:T(8,128)} copy(f32[128,8,256]{2,1,0:T(8,128)S(1)} %get-tuple-element.4) | data formatting | bytes 2097152
  74.8 0.7 copy.8
Async XLA Ops:
  0.6 0.7 copy-start.2
  1.3 1.2 %copy-start = (f32[2,8,16384]{2,1,0:T(8,128)S(1)}, f32[2,8,16384]{2,1,0:T(8,128)}, u32[]{:S(2)}) copy-start(f32[2,8,16384]{2,1,0:T(8,128)} %param.3) | copy-start | bytes 3145732
  2.5 1.0 %copy-start.1 = (f32[2,1,256,256]{3,2,1,0:T(8,128)S(1)}, f32[2,1,256,256]{3,2,1,0:T(8,128)}, u32[]{:S(2)}) copy-start(f32[2,1,256,256]{3,2,1,0:T(8,128)} %rot_ref.1) | copy-start | bytes 1572868

commit v2 on v1

--- a/solution.py
+++ b/solution.py
@@ -27,24 +27,36 @@
 
 def kernel(
     sizes,
+    order_hbm,
+    x_hbm,
+    rot_hbm,
+    out_ref,
+    gram_ref,
     order_ref,
     x_ref,
     rot_ref,
-    out_ref,
-    gram_ref,
+    rot_before,
     stage,
     blocks,
+    extra,
     first,
     second,
     arrived,
     result,
     rot_high,
     rot_low,
+    before_high,
+    before_low,
     sums,
     shares,
     share_in,
+    load_sem,
     a2a_send,
     a2a_recv,
+    extra_send,
+    extra_recv,
+    before_send,
+    before_recv,
     next_send,
     next_recv,
     out_sem,
@@ -63,6 +75,17 @@
     row = lax.axis_index("row")
     my_group = me // per_group
     after = (me + 1) % snaps
+    run = snaps // 2
+    is_head = me % run == 0
+    is_last = me % run == run - 1
+
+    loads = [
+        pltpu.make_async_copy(order_hbm, order_ref, load_sem.at[0]),
+        pltpu.make_async_copy(x_hbm, x_ref, load_sem.at[1]),
+        pltpu.make_async_copy(rot_hbm, rot_ref, load_sem.at[2]),
+    ]
+    for load in loads:
+        load.start()
 
     barrier = pltpu.get_barrier_semaphore()
 
@@ -76,6 +99,9 @@
         pl.semaphore_signal(
             barrier, inc=1, device_id={"snap": me, "row": (row + i) % rows}, device_id_type=MESH
         )
+
+    for load in loads:
+        load.wait()
 
     @pl.loop(0, snaps, unroll=4)
     def _(d):
@@ -89,7 +115,24 @@
     sums[...] = jnp.zeros_like(sums)
     blocks[pl.ds(me * modes, modes)] = stage[me]
 
+    @pl.when(is_head)
+    def _():
+        extra[pl.ds(me * modes, modes)] = stage[(me + snaps - 1) % snaps]
+
     pl.semaphore_wait(barrier, snaps - 1 + rows - 1)
+
+    before_copy = pltpu.make_async_remote_copy(
+        src_ref=rot_ref.at[0, 0, :, pl.ds(half, half)],
+        dst_ref=rot_before,
+        send_sem=before_send,
+        recv_sem=before_recv,
+        device_id={"snap": after, "row": row},
+        device_id_type=MESH,
+    )
+
+    @pl.when(is_last)
+    def _():
+        before_copy.start()
 
     def send_blocks(d):
         pltpu.make_async_remote_copy(
@@ -101,8 +144,18 @@
             device_id_type=MESH,
         ).start()
 
-    low_part = me % (snaps // 2)
-    high_part = me // (snaps // 2)
+        @pl.when(d % run == 0)
+        def _():
+            pltpu.make_async_remote_copy(
+                src_ref=stage.at[(d + snaps - 1) % snaps],
+                dst_ref=extra.at[pl.ds(me * modes, modes)],
+                send_sem=extra_send,
+                recv_sem=extra_recv.at[my_group],
+                device_id={"snap": d, "row": row},
+                device_id_type=MESH,
+            ).start()
+
+    high_part = me // run
     ys = GROUPS // 2
     my_y = my_group % ys
     my_place = me % per_group
@@ -112,23 +165,30 @@
         @pl.loop(0, per_group)
         def _(j):
             place = ((my_y + k) % ys) * per_group + (my_place + j) % per_group
-            send_blocks((1 - high_part) * (snaps // 2) + place)
+            send_blocks((1 - high_part) * run + place)
 
             @pl.when(k + j > 0)
             def _():
-                send_blocks(high_part * (snaps // 2) + place)
-
-    def wait_group(group):
-        whole = blocks.at[pl.ds(0, group_modes)]
-        part = blocks.at[pl.ds(0, group_modes - modes)]
+                send_blocks(high_part * run + place)
+
+    def wait_group(buffer, sems, group):
+        whole = buffer.at[pl.ds(0, group_modes)]
+        part = buffer.at[pl.ds(0, group_modes - modes)]
 
         @pl.when(group == my_group)
         def _():
-            pltpu.make_async_copy(part, part, a2a_recv.at[group]).wait()
+            pltpu.make_async_copy(part, part, sems.at[group]).wait()
 
         @pl.when(group != my_group)
         def _():
-            pltpu.make_async_copy(whole, whole, a2a_recv.at[group]).wait()
+            pltpu.make_async_copy(whole, whole, sems.at[group]).wait()
+
+    @pl.when(is_head)
+    def _():
+        before_copy.wait_recv()
+        high, low = split(rot_before[...])
+        before_high[...] = high
+        before_low[...] = low
 
     def turn(r, matrix):
         high, low = split(matrix)
@@ -156,19 +216,35 @@
     def round_one(k):
         group = group_at(k, 0)
         span = pl.ds(group * group_modes, group_modes)
-        wait_group(group)
+        wait_group(blocks, a2a_recv, group)
         turned = turn(0, blocks[span].reshape(group_rows, width))
         turned = turned.reshape(group_modes, delays, width)
         first[span] = turned[:, :, :half]
         second[span] = turned[:, :, half:]
-        send_next(group).start()
-
-    wraps = jnp.where(my_place == 0, 1, 0)
+
+        @pl.when(jnp.logical_not(is_last))
+        def _():
+            send_next(group).start()
+
+        @pl.when(is_head)
+        def _():
+            wait_group(extra, extra_recv, group)
+            high, low = split(extra[span].reshape(group_rows, width))
+            turned = dot(high, before_high[...]) + (
+                dot(high, before_low[...]) + dot(low, before_high[...])
+            )
+            arrived[span] = turned.reshape(group_modes, delays, half)
+
+    wraps = jnp.where(jnp.logical_and(my_place == 0, jnp.logical_not(is_head)), 1, 0)
 
     def round_two(k):
         group = group_at(k, wraps)
         span = pl.ds(group * group_modes, group_modes)
-        send_next(group).wait_recv()
+
+        @pl.when(jnp.logical_not(is_head))
+        def _():
+            send_next(group).wait_recv()
+
         matrix = jnp.concatenate([first[span], arrived[span]], axis=2)
         turned = turn(1, matrix.reshape(group_rows, width))
         result[span] = turned.reshape(group_modes, delays, width)
@@ -213,7 +289,25 @@
     collect(0)
     everything = stage.at[pl.ds(0, snaps - 1)]
     pltpu.make_async_copy(everything, everything, a2a_send).wait()
-    pltpu.make_async_copy(second, second, next_send).wait()
+    two = stage.at[pl.ds(0, 2)]
+    one = stage.at[0]
+
+    @pl.when(is_head)
+    def _():
+        pltpu.make_async_copy(one, one, extra_send).wait()
+
+    @pl.when(jnp.logical_not(is_head))
+    def _():
+        pltpu.make_async_copy(two, two, extra_send).wait()
+
+    @pl.when(is_last)
+    def _():
+        before_copy.wait_send()
+
+    @pl.when(jnp.logical_not(is_last))
+    def _():
+        pltpu.make_async_copy(second, second, next_send).wait()
+
     pltpu.make_async_copy(result, out_ref, out_sem).wait()
     collect(1)
 
@@ -229,16 +323,22 @@
     f32, bf16 = jnp.float32, jnp.bfloat16
     blocks = delay_matrix.reshape(modes, delays, 2 * snaps, half).transpose(0, 2, 1, 3)
     vmem = pl.BlockSpec(memory_space=pltpu.VMEM)
+    hbm = pl.BlockSpec(memory_space=pltpu.HBM)
     return pl.pallas_call(
         functools.partial(kernel, sizes),
         out_shape=(
             jax.ShapeDtypeStruct((snaps * modes, delays, width), f32),
             jax.ShapeDtypeStruct((2, 1, share_rows, width), f32),
         ),
-        in_specs=[pl.BlockSpec(memory_space=pltpu.SMEM), vmem, vmem],
-        out_specs=(pl.BlockSpec(memory_space=pl.ANY), vmem),
+        in_specs=[hbm, hbm, hbm],
+        out_specs=(hbm, vmem),
         scratch_shapes=[
+            pltpu.SMEM(arrangement.shape, arrangement.dtype),
+            pltpu.VMEM(blocks.shape, f32),
+            pltpu.VMEM(rotations.shape, f32),
+            pltpu.VMEM((width, half), f32),
             pltpu.VMEM((snaps, modes, delays, width), f32),
+            pltpu.VMEM((snaps * modes, delays, width), f32),
             pltpu.VMEM((snaps * modes, delays, width), f32),
             pltpu.VMEM((snaps * modes, delays, half), f32),
             pltpu.VMEM((snaps * modes, delays, half), f32),
@@ -246,11 +346,18 @@
             pltpu.VMEM((snaps * modes, delays, width), f32),
             pltpu.VMEM((2, width, width), bf16),
             pltpu.VMEM((2, width, width), bf16),
+            pltpu.VMEM((width, half), bf16),
+            pltpu.VMEM((width, half), bf16),
             pltpu.VMEM((2, width, 2 * width), f32),
             pltpu.VMEM((2, rows, share_rows, width), f32),
             pltpu.VMEM((2, rows, share_rows, width), f32),
+            pltpu.SemaphoreType.DMA((3,)),
             pltpu.SemaphoreType.DMA,
             pltpu.SemaphoreType.DMA((GROUPS,)),
+            pltpu.SemaphoreType.DMA,
+            pltpu.SemaphoreType.DMA((GROUPS,)),
+            pltpu.SemaphoreType.DMA,
+            pltpu.SemaphoreType.DMA,
             pltpu.SemaphoreType.DMA,
             pltpu.SemaphoreType.DMA((GROUPS,)),
             pltpu.SemaphoreType.DMA,
@@ -258,7 +365,7 @@
             pltpu.SemaphoreType.DMA((2, rows)),
         ],
         compiler_params=pltpu.CompilerParams(
-            collective_id=0, has_side_effects=True, vmem_limit_bytes=32 * 1024 * 1024
+            collective_id=0, has_side_effects=True, vmem_limit_bytes=60 * 1024 * 1024
         ),
         name="rounds",
     )(arrangement, blocks, rotations)

time: 75.8 us -> 58.6 us (0.77)
  the two profiles are of different devices: /device:TPU:224 before, /device:TPU:1 now
where the time goes in v2:
time: 58.6 us; the launch traced here: 58.5 us
  Pallas kernels  54.9 us (94%)
  local copies, waits for them, and re-layouts  2.96 us (5%)
  between operations  0.65 us (1%)
    pallas_call x1, Pallas kernels, body(): pl.pallas_call(functools.partial(kernel, sizes), out_shape=(jax.ShapeDtyp...  54.9 us
    unnamed x4, local copies, waits for them, and re-layouts  2.96 us

profile of v2, /device:TPU:1, one launch (start us, length us, event | category | flops | bytes accessed | tf_op | source)
XLA Modules:
  0.0 58.5 jit_solution(8028629145973581543)
XLA Ops:
  0.6 54.9 %rounds.1 = (f32[128,8,256]{2,1,0:T(8,128)}, f32[2,1,64,256]{3,2,1,0:T(8,128)}) custom-call(s32[128]{0:T(128)} %order_hbm.1, f32[2,128,8,128]{3,2,1,0:T(8,128)} %bitcast.3, f32[2,1,256,256]{3,2,1,0:T(8,128)} %rot_hbm.1), custom_call_target="tpu_custom_call" | custom-call | tf_op jit(solution)/shard_map/rounds/pallas_call | solution.py:327
  55.5 0.0 copy-start
  55.5 2.3 %copy.7 = f32[128,8,256]{2,1,0:T(8,128)} copy(f32[128,8,256]{2,1,0:T(8,128)} %get-tuple-element.4) | data formatting | bytes 2097152
  57.8 0.0 copy-done
  57.8 0.7 %copy.8 = f32[2,1,64,256]{3,2,1,0:T(8,128)} copy(f32[2,1,64,256]{3,2,1,0:T(8,128)S(1)} %copy-done) | data formatting | bytes 262144
Async XLA Ops:
  55.5 2.3 %copy-start = (f32[2,1,64,256]{3,2,1,0:T(8,128)S(1)}, f32[2,1,64,256]{3,2,1,0:T(8,128)}, u32[]{:S(2)}) copy-start(f32[2,1,64,256]{3,2,1,0:T(8,128)} %get-tuple-element.5) | copy-start | bytes 393220

commit v3 on v2

--- a/solution.py
+++ b/solution.py
@@ -8,6 +8,7 @@
 from jax.sharding import PartitionSpec as P
 
 MESH = pl.DeviceIdType.MESH
+RELAY_LAG = 2
 GROUPS = 8
 
 
@@ -31,17 +32,19 @@
     x_hbm,
     rot_hbm,
     out_ref,
-    gram_ref,
+    gram_out,
     order_ref,
     x_ref,
     rot_ref,
     rot_before,
     stage,
+    extra_stage,
     blocks,
     extra,
     first,
     second,
     arrived,
+    relayed,
     result,
     rot_high,
     rot_low,
@@ -50,6 +53,7 @@
     sums,
     shares,
     share_in,
+    gram_ref,
     load_sem,
     a2a_send,
     a2a_recv,
@@ -59,7 +63,10 @@
     before_recv,
     next_send,
     next_recv,
+    relay_send,
+    relay_recv,
     out_sem,
+    gram_sem,
     share_send,
     share_recv,
 ):
@@ -76,8 +83,11 @@
     my_group = me // per_group
     after = (me + 1) % snaps
     run = snaps // 2
+    high_part = me // run
     is_head = me % run == 0
     is_last = me % run == run - 1
+    in_low, in_high = high_part == 0, high_part == 1
+    hands_over = jnp.logical_and(is_last, in_high)
 
     loads = [
         pltpu.make_async_copy(order_hbm, order_ref, load_sem.at[0]),
@@ -102,22 +112,6 @@
 
     for load in loads:
         load.wait()
-
-    @pl.loop(0, snaps, unroll=4)
-    def _(d):
-        stage[d, :, :, :half] = x_ref[:, order_ref[2 * d]]
-        stage[d, :, :, half:] = x_ref[:, order_ref[2 * d + 1]]
-
-    for r in range(2):
-        high, low = split(rot_ref[r, 0])
-        rot_high[r] = high
-        rot_low[r] = low
-    sums[...] = jnp.zeros_like(sums)
-    blocks[pl.ds(me * modes, modes)] = stage[me]
-
-    @pl.when(is_head)
-    def _():
-        extra[pl.ds(me * modes, modes)] = stage[(me + snaps - 1) % snaps]
 
     pl.semaphore_wait(barrier, snaps - 1 + rows - 1)
 
@@ -135,6 +129,8 @@
         before_copy.start()
 
     def send_blocks(d):
+        stage[d, :, :, :half] = x_ref[:, order_ref[2 * d]]
+        stage[d, :, :, half:] = x_ref[:, order_ref[2 * d + 1]]
         pltpu.make_async_remote_copy(
             src_ref=stage.at[d],
             dst_ref=blocks.at[pl.ds(me * modes, modes)],
@@ -144,32 +140,60 @@
             device_id_type=MESH,
         ).start()
 
-        @pl.when(d % run == 0)
-        def _():
-            pltpu.make_async_remote_copy(
-                src_ref=stage.at[(d + snaps - 1) % snaps],
-                dst_ref=extra.at[pl.ds(me * modes, modes)],
-                send_sem=extra_send,
-                recv_sem=extra_recv.at[my_group],
-                device_id={"snap": d, "row": row},
-                device_id_type=MESH,
-            ).start()
-
-    high_part = me // run
+        @pl.when(jnp.logical_or(d == run, d == high_part * run))
+        def _():
+            send_extra(d)
+
+    def send_extra(head):
+        before = (head + snaps - 1) % snaps
+        place = head // run
+        extra_stage[place, :, :, :half] = x_ref[:, order_ref[2 * before]]
+        extra_stage[place, :, :, half:] = x_ref[:, order_ref[2 * before + 1]]
+        pltpu.make_async_remote_copy(
+            src_ref=extra_stage.at[place],
+            dst_ref=extra.at[pl.ds(me * modes, modes)],
+            send_sem=extra_send,
+            recv_sem=extra_recv.at[my_group],
+            device_id={"snap": head, "row": row},
+            device_id_type=MESH,
+        ).start()
+
     ys = GROUPS // 2
     my_y = my_group % ys
     my_place = me % per_group
 
-    @pl.loop(0, ys)
-    def _(k):
-        @pl.loop(0, per_group)
-        def _(j):
-            place = ((my_y + k) % ys) * per_group + (my_place + j) % per_group
-            send_blocks((1 - high_part) * run + place)
-
-            @pl.when(k + j > 0)
+    def place_at(i):
+        k, j = i // per_group, i % per_group
+        return ((my_y + k) % ys) * per_group + (my_place + j) % per_group
+
+    @pl.loop(0, run)
+    def _(i):
+        send_blocks((1 - high_part) * run + place_at(i))
+
+        @pl.when(2 * i < run)
+        def _():
+            @pl.when(i > 0)
             def _():
-                send_blocks(high_part * run + place)
+                send_blocks(high_part * run + place_at(2 * i))
+
+            send_blocks(high_part * run + place_at(2 * i + 1))
+
+    stage[me, :, :, :half] = x_ref[:, order_ref[2 * me]]
+    stage[me, :, :, half:] = x_ref[:, order_ref[2 * me + 1]]
+    blocks[pl.ds(me * modes, modes)] = stage[me]
+
+
+    @pl.when(is_head)
+    def _():
+        before = (me + snaps - 1) % snaps
+        extra[pl.ds(me * modes, modes), :, :half] = x_ref[:, order_ref[2 * before]]
+        extra[pl.ds(me * modes, modes), :, half:] = x_ref[:, order_ref[2 * before + 1]]
+
+    for r in range(2):
+        high, low = split(rot_ref[r, 0])
+        rot_high[r] = high
+        rot_low[r] = low
+    sums[...] = jnp.zeros_like(sums)
 
     def wait_group(buffer, sems, group):
         whole = buffer.at[pl.ds(0, group_modes)]
@@ -183,20 +207,14 @@
         def _():
             pltpu.make_async_copy(whole, whole, sems.at[group]).wait()
 
-    @pl.when(is_head)
-    def _():
-        before_copy.wait_recv()
-        high, low = split(rot_before[...])
-        before_high[...] = high
-        before_low[...] = low
-
     def turn(r, matrix):
         high, low = split(matrix)
-        turned = dot(high, rot_high[r]) + (dot(high, rot_low[r]) + dot(low, rot_high[r]))
+        return dot(high, rot_high[r]) + (dot(high, rot_low[r]) + dot(low, rot_high[r]))
+
+    def add_gram(r, turned):
         high, low = split(turned)
         sums[r, :, :width] += dot_rows(high, high)
         sums[r, :, width:] += dot_rows(high, low)
-        return turned
 
     def send_next(group):
         span = pl.ds(group * group_modes, group_modes)
@@ -209,24 +227,82 @@
             device_id_type=MESH,
         )
 
-    def group_at(k, turned_by):
-        part = (high_part + k // ys) % 2
-        return part * ys + (my_y + ys - (k + turned_by) % ys) % ys
+    def to_relay(group, step):
+        return pltpu.make_async_remote_copy(
+            src_ref=second.at[pl.ds(group * group_modes, group_modes)],
+            dst_ref=relayed,
+            send_sem=next_send,
+            recv_sem=relay_recv,
+            device_id={"snap": me - step * per_group, "row": row},
+            device_id_type=MESH,
+        )
+
+    relay_step = ys - 1 - my_y
+    is_relay = jnp.logical_and(my_place == per_group - 1, jnp.logical_and(in_high, relay_step > 0))
+    relay_group = high_part * ys + ys - 1 - relay_step
+    relay_out = pltpu.make_async_remote_copy(
+        src_ref=relayed,
+        dst_ref=arrived.at[pl.ds(relay_group * group_modes, group_modes)],
+        send_sem=relay_send,
+        recv_sem=next_recv.at[relay_group],
+        device_id={"snap": (high_part * run + run) % snaps, "row": row},
+        device_id_type=MESH,
+    )
+
+    def pass_on(k):
+        @pl.when(jnp.logical_and(is_relay, k == relay_step + RELAY_LAG))
+        def _():
+            pltpu.make_async_copy(relayed, relayed, relay_recv).wait()
+            relay_out.start()
+
+    def group_of(crossing, k):
+        return (high_part + crossing) % 2 * ys + (my_y + ys - k % ys) % ys
+
+    def in_order(i):
+        crossing = jnp.where(jnp.logical_or(i == 2, i >= 5), 1, 0)
+        before = jnp.where(i >= 5, i - 4, jnp.where(i == 2, 0, jnp.where(i > 2, i - 1, i)))
+        return crossing, before
 
     def round_one(k):
-        group = group_at(k, 0)
+        group = group_of(*in_order(k))
         span = pl.ds(group * group_modes, group_modes)
         wait_group(blocks, a2a_recv, group)
         turned = turn(0, blocks[span].reshape(group_rows, width))
-        turned = turned.reshape(group_modes, delays, width)
-        first[span] = turned[:, :, :half]
-        second[span] = turned[:, :, half:]
-
-        @pl.when(jnp.logical_not(is_last))
+        first[span] = turned[:, :half].reshape(group_modes, delays, half)
+        second[span] = turned[:, half:].reshape(group_modes, delays, half)
+        crossing, step = in_order(k)
+
+        @pl.when(jnp.logical_or(jnp.logical_not(is_last), jnp.logical_and(hands_over, crossing + step == 0)))
         def _():
             send_next(group).start()
 
-        @pl.when(is_head)
+        @pl.when(jnp.logical_and(hands_over, jnp.logical_and(crossing == 0, step > 0)))
+        def _():
+            to_relay(group, step).start()
+
+        add_gram(0, turned)
+
+    wraps = jnp.logical_and(my_place == 0, me != run)
+
+    def round_two(k):
+        @pl.when(jnp.logical_and(is_head, k == 0))
+        def _():
+            before_copy.wait_recv()
+            high, low = split(rot_before[...])
+            before_high[...] = high
+            before_low[...] = low
+
+        crossing, step = in_order(k)
+        group = jnp.where(wraps, group_of(k // ys, k % ys + 1), group_of(crossing, step))
+        span = pl.ds(group * group_modes, group_modes)
+
+        raw = jnp.logical_and(is_head, jnp.logical_or(in_high, group // ys == 0))
+
+        @pl.when(jnp.logical_not(raw))
+        def _():
+            send_next(group).wait_recv()
+
+        @pl.when(raw)
         def _():
             wait_group(extra, extra_recv, group)
             high, low = split(extra[span].reshape(group_rows, width))
@@ -235,20 +311,11 @@
             )
             arrived[span] = turned.reshape(group_modes, delays, half)
 
-    wraps = jnp.where(jnp.logical_and(my_place == 0, jnp.logical_not(is_head)), 1, 0)
-
-    def round_two(k):
-        group = group_at(k, wraps)
-        span = pl.ds(group * group_modes, group_modes)
-
-        @pl.when(jnp.logical_not(is_head))
-        def _():
-            send_next(group).wait_recv()
-
         matrix = jnp.concatenate([first[span], arrived[span]], axis=2)
         turned = turn(1, matrix.reshape(group_rows, width))
         result[span] = turned.reshape(group_modes, delays, width)
         pltpu.make_async_copy(result.at[span], out_ref.at[span], out_sem).start()
+        add_gram(1, turned)
 
     def finish(r):
         cross = sums[r, :, width:]
@@ -275,34 +342,46 @@
         for i in range(1, rows):
             total = total + share_in[r, i]
         gram_ref[r, 0] = total
+        pltpu.make_async_copy(gram_ref.at[r], gram_out.at[r], gram_sem.at[r]).start()
 
     round_one(0)
-
-    @pl.loop(1, GROUPS)
+    round_one(1)
+
+    @pl.loop(2, GROUPS)
     def _(k):
+        pass_on(k)
         round_one(k)
-        round_two(k - 1)
+        round_two(k - 2)
 
     finish(0)
+    round_two(GROUPS - 2)
     round_two(GROUPS - 1)
     finish(1)
     collect(0)
     everything = stage.at[pl.ds(0, snaps - 1)]
     pltpu.make_async_copy(everything, everything, a2a_send).wait()
-    two = stage.at[pl.ds(0, 2)]
-    one = stage.at[0]
-
-    @pl.when(is_head)
+    one = extra_stage.at[0]
+
+    @pl.when(jnp.logical_and(in_low, me > 0))
+    def _():
+        pltpu.make_async_copy(extra_stage, extra_stage, extra_send).wait()
+
+    @pl.when(jnp.logical_or(me == 0, me > run))
     def _():
         pltpu.make_async_copy(one, one, extra_send).wait()
 
-    @pl.when(jnp.logical_not(is_head))
-    def _():
-        pltpu.make_async_copy(two, two, extra_send).wait()
+    @pl.when(is_relay)
+    def _():
+        relay_out.wait_send()
 
     @pl.when(is_last)
     def _():
         before_copy.wait_send()
+
+    @pl.when(hands_over)
+    def _():
+        sent = second.at[pl.ds(0, run * modes)]
+        pltpu.make_async_copy(sent, sent, next_send).wait()
 
     @pl.when(jnp.logical_not(is_last))
     def _():
@@ -310,6 +389,25 @@
 
     pltpu.make_async_copy(result, out_ref, out_sem).wait()
     collect(1)
+    for r in range(2):
+        pltpu.make_async_copy(gram_ref.at[r], gram_out.at[r], gram_sem.at[r]).wait()
+
+
+def write_results(out_from, gram_from, out_ref, gram_ref, out_held, gram_held, in_sem, out_sem):
+    pieces = in_sem.shape[0] - 1
+    length = out_ref.shape[0] // pieces
+    spans = [pl.ds(i * length, length) for i in range(pieces)]
+    steps = [(out_from.at[span], out_held.at[span], out_ref.at[span]) for span in spans]
+    steps.append((gram_from, gram_held, gram_ref))
+    loads = [pltpu.make_async_copy(a, b, in_sem.at[i]) for i, (a, b, _) in enumerate(steps)]
+    stores = [pltpu.make_async_copy(b, c, out_sem.at[i]) for i, (_, b, c) in enumerate(steps)]
+    for load in loads:
+        load.start()
+    for load, store in zip(loads, stores):
+        load.wait()
+        store.start()
+    for store in stores:
+        store.wait()
 
 
 def body(delay_matrix, arrangement, rotations):
@@ -322,27 +420,29 @@
     sizes = (snaps, rows, modes, delays, width)
     f32, bf16 = jnp.float32, jnp.bfloat16
     blocks = delay_matrix.reshape(modes, delays, 2 * snaps, half).transpose(0, 2, 1, 3)
-    vmem = pl.BlockSpec(memory_space=pltpu.VMEM)
     hbm = pl.BlockSpec(memory_space=pltpu.HBM)
-    return pl.pallas_call(
+    out_shape = (
+        jax.ShapeDtypeStruct((snaps * modes, delays, width), f32),
+        jax.ShapeDtypeStruct((2, 1, share_rows, width), f32),
+    )
+    rotated, grams = pl.pallas_call(
         functools.partial(kernel, sizes),
-        out_shape=(
-            jax.ShapeDtypeStruct((snaps * modes, delays, width), f32),
-            jax.ShapeDtypeStruct((2, 1, share_rows, width), f32),
-        ),
+        out_shape=out_shape,
         in_specs=[hbm, hbm, hbm],
-        out_specs=(hbm, vmem),
+        out_specs=(hbm, hbm),
         scratch_shapes=[
             pltpu.SMEM(arrangement.shape, arrangement.dtype),
             pltpu.VMEM(blocks.shape, f32),
             pltpu.VMEM(rotations.shape, f32),
             pltpu.VMEM((width, half), f32),
             pltpu.VMEM((snaps, modes, delays, width), f32),
+            pltpu.VMEM((2, modes, delays, width), f32),
             pltpu.VMEM((snaps * modes, delays, width), f32),
             pltpu.VMEM((snaps * modes, delays, width), f32),
             pltpu.VMEM((snaps * modes, delays, half), f32),
             pltpu.VMEM((snaps * modes, delays, half), f32),
             pltpu.VMEM((snaps * modes, delays, half), f32),
+            pltpu.VMEM((snaps // GROUPS * modes, delays, half), f32),
             pltpu.VMEM((snaps * modes, delays, width), f32),
             pltpu.VMEM((2, width, width), bf16),
             pltpu.VMEM((2, width, width), bf16),
@@ -351,6 +451,7 @@
             pltpu.VMEM((2, width, 2 * width), f32),
             pltpu.VMEM((2, rows, share_rows, width), f32),
             pltpu.VMEM((2, rows, share_rows, width), f32),
+            pltpu.VMEM((2, 1, share_rows, width), f32),
             pltpu.SemaphoreType.DMA((3,)),
             pltpu.SemaphoreType.DMA,
             pltpu.SemaphoreType.DMA((GROUPS,)),
@@ -361,6 +462,9 @@
             pltpu.SemaphoreType.DMA,
             pltpu.SemaphoreType.DMA((GROUPS,)),
             pltpu.SemaphoreType.DMA,
+            pltpu.SemaphoreType.DMA,
+            pltpu.SemaphoreType.DMA,
+            pltpu.SemaphoreType.DMA((2,)),
             pltpu.SemaphoreType.DMA((2, rows)),
             pltpu.SemaphoreType.DMA((2, rows)),
         ],
@@ -369,6 +473,20 @@
         ),
         name="rounds",
     )(arrangement, blocks, rotations)
+    return pl.pallas_call(
+        write_results,
+        out_shape=out_shape,
+        in_specs=[hbm, hbm],
+        out_specs=(hbm, hbm),
+        scratch_shapes=[
+            pltpu.VMEM(out_shape[0].shape, f32),
+            pltpu.VMEM(out_shape[1].shape, f32),
+            pltpu.SemaphoreType.DMA((9,)),
+            pltpu.SemaphoreType.DMA((9,)),
+        ],
+        compiler_params=pltpu.CompilerParams(vmem_limit_bytes=60 * 1024 * 1024),
+        name="write_results",
+    )(rotated, grams)
 
 
 def solution(mesh):

time: 58.6 us -> 55.8 us (0.952)
  the two profiles are of different devices: /device:TPU:1 before, /device:TPU:32 now
where the time goes in v3:
time: 55.8 us; the launch traced here: 55.7 us
  Pallas kernels  55.1 us (99%)
  between operations  0.64 us (1%)
    pallas_call x1, Pallas kernels, body(): pl.pallas_call(functools.partial(kernel, sizes), out_shape=out_shape, in_...  52.9 us
    pallas_call x1, Pallas kernels, body(): pl.pallas_call(write_results, out_shape=out_shape, in_specs=[hbm, hbm], o...  2.15 us

profile of v3, /device:TPU:32, one launch (start us, length us, event | category | flops | bytes accessed | tf_op | source)
XLA Modules:
  0.0 55.7 jit_solution(8499230555507651208)
XLA Ops:
  0.6 52.9 %rounds.1 = (f32[128,8,256]{2,1,0:T(8,128)}, f32[2,1,64,256]{3,2,1,0:T(8,128)}) custom-call(s32[128]{0:T(128)} %order_hbm.1, f32[2,128,8,128]{3,2,1,0:T(8,128)} %bitcast.3, f32[2,1,256,256]{3,2,1,0:T(8,128)} %rot_hbm.1), custom_call_target="tpu_custom_call" | custom-call | tf_op jit(solution)/shard_map/rounds/pallas_call | solution.py:428
  53.6 2.1 %write_results.1 = (f32[128,8,256]{2,1,0:T(8,128)}, f32[2,1,64,256]{3,2,1,0:T(8,128)}) custom-call(f32[128,8,256]{2,1,0:T(8,128)} %get-tuple-element.4.out_from, f32[2,1,64,256]{3,2,1,0:T(8,128)} %get-tuple-element.5.gram_from), custom_call_target="tpu_custom_call" | custom-call | tf_op jit(solution)/shard_map/write_results/pallas_call | solution.py:476

commit v4 on v3

--- a/solution.py
+++ b/solution.py
@@ -8,7 +8,6 @@
 from jax.sharding import PartitionSpec as P
 
 MESH = pl.DeviceIdType.MESH
-RELAY_LAG = 2
 GROUPS = 8
 
 
@@ -44,7 +43,6 @@
     first,
     second,
     arrived,
-    relayed,
     result,
     rot_high,
     rot_low,
@@ -63,12 +61,14 @@
     before_recv,
     next_send,
     next_recv,
-    relay_send,
-    relay_recv,
     out_sem,
     gram_sem,
     share_send,
     share_recv,
+    uppers_in,
+    all_in,
+    rows_in,
+    rows_all_in,
 ):
     snaps, rows, modes, delays, width = sizes
     half = width // 2
@@ -83,11 +83,8 @@
     my_group = me // per_group
     after = (me + 1) % snaps
     run = snaps // 2
-    high_part = me // run
     is_head = me % run == 0
     is_last = me % run == run - 1
-    in_low, in_high = high_part == 0, high_part == 1
-    hands_over = jnp.logical_and(is_last, in_high)
 
     loads = [
         pltpu.make_async_copy(order_hbm, order_ref, load_sem.at[0]),
@@ -97,23 +94,25 @@
     for load in loads:
         load.start()
 
+    high_part = me // run
+    in_low = high_part == 0
+    in_high = high_part == 1
+    across = (me + run) % snaps
     barrier = pltpu.get_barrier_semaphore()
 
-    @pl.loop(1, snaps)
-    def _(i):
+    def signal(semaphore, snap, to_row):
         pl.semaphore_signal(
-            barrier, inc=1, device_id={"snap": (me + i) % snaps, "row": row}, device_id_type=MESH
+            semaphore, inc=1, device_id={"snap": snap, "row": to_row}, device_id_type=MESH
         )
 
-    for i in range(1, rows):
-        pl.semaphore_signal(
-            barrier, inc=1, device_id={"snap": me, "row": (row + i) % rows}, device_id_type=MESH
-        )
-
-    for load in loads:
-        load.wait()
-
-    pl.semaphore_wait(barrier, snaps - 1 + rows - 1)
+    @pl.when(in_low)
+    def _():
+        @pl.loop(1, run)
+        def _(i):
+            signal(barrier, (me + i) % run, row)
+
+        for i in range(1, rows):
+            signal(barrier, me, (row + i) % rows)
 
     before_copy = pltpu.make_async_remote_copy(
         src_ref=rot_ref.at[0, 0, :, pl.ds(half, half)],
@@ -124,7 +123,23 @@
         device_id_type=MESH,
     )
 
-    @pl.when(is_last)
+    @pl.when(in_low)
+    def _():
+        pl.semaphore_wait(barrier, run - 1 + rows - 1)
+        signal(barrier, across, row)
+
+    @pl.when(in_high)
+    def _():
+        pl.semaphore_wait(barrier, 1)
+
+        @pl.loop(0, run)
+        def _(i):
+            signal(uppers_in, (me + i) % run, row)
+
+    for load in loads:
+        load.wait()
+
+    @pl.when(jnp.logical_and(in_high, is_last))
     def _():
         before_copy.start()
 
@@ -140,7 +155,7 @@
             device_id_type=MESH,
         ).start()
 
-        @pl.when(jnp.logical_or(d == run, d == high_part * run))
+        @pl.when(d % run == 0)
         def _():
             send_extra(d)
 
@@ -162,21 +177,51 @@
     my_y = my_group % ys
     my_place = me % per_group
 
-    def place_at(i):
-        k, j = i // per_group, i % per_group
+    def place_at(k, j):
         return ((my_y + k) % ys) * per_group + (my_place + j) % per_group
 
-    @pl.loop(0, run)
-    def _(i):
-        send_blocks((1 - high_part) * run + place_at(i))
-
-        @pl.when(2 * i < run)
-        def _():
-            @pl.when(i > 0)
+    def send_part(k, j, part):
+        to = part * run + place_at(k, j)
+
+        @pl.when(to != me)
+        def _():
+            send_blocks(to)
+
+    @pl.loop(0, jnp.where(in_low, ys, 1))
+    def _(k):
+        @pl.loop(0, per_group)
+        def _(j):
+            send_part(k, j, 0)
+
+    @pl.when(in_low)
+    def _():
+        pl.semaphore_wait(uppers_in, run)
+        signal(all_in, across, row)
+        for i in range(1, rows):
+            signal(rows_in, me, (row + i) % rows)
+
+        @pl.when(is_last)
+        def _():
+            before_copy.start()
+
+    @pl.when(in_high)
+    def _():
+        pl.semaphore_wait(all_in, 1)
+
+    @pl.loop(0, ys)
+    def _(k):
+        @pl.loop(0, per_group)
+        def _(j):
+            @pl.when(jnp.logical_and(in_high, k > 0))
             def _():
-                send_blocks(high_part * run + place_at(2 * i))
-
-            send_blocks(high_part * run + place_at(2 * i + 1))
+                send_part(k, j, 0)
+
+            send_part(k, j, 1)
+
+    @pl.when(in_low)
+    def _():
+        pl.semaphore_wait(rows_in, rows - 1)
+        signal(rows_all_in, across, row)
 
     stage[me, :, :, :half] = x_ref[:, order_ref[2 * me]]
     stage[me, :, :, half:] = x_ref[:, order_ref[2 * me + 1]]
@@ -227,62 +272,25 @@
             device_id_type=MESH,
         )
 
-    def to_relay(group, step):
-        return pltpu.make_async_remote_copy(
-            src_ref=second.at[pl.ds(group * group_modes, group_modes)],
-            dst_ref=relayed,
-            send_sem=next_send,
-            recv_sem=relay_recv,
-            device_id={"snap": me - step * per_group, "row": row},
-            device_id_type=MESH,
-        )
-
-    relay_step = ys - 1 - my_y
-    is_relay = jnp.logical_and(my_place == per_group - 1, jnp.logical_and(in_high, relay_step > 0))
-    relay_group = high_part * ys + ys - 1 - relay_step
-    relay_out = pltpu.make_async_remote_copy(
-        src_ref=relayed,
-        dst_ref=arrived.at[pl.ds(relay_group * group_modes, group_modes)],
-        send_sem=relay_send,
-        recv_sem=next_recv.at[relay_group],
-        device_id={"snap": (high_part * run + run) % snaps, "row": row},
-        device_id_type=MESH,
-    )
-
-    def pass_on(k):
-        @pl.when(jnp.logical_and(is_relay, k == relay_step + RELAY_LAG))
-        def _():
-            pltpu.make_async_copy(relayed, relayed, relay_recv).wait()
-            relay_out.start()
-
-    def group_of(crossing, k):
-        return (high_part + crossing) % 2 * ys + (my_y + ys - k % ys) % ys
-
-    def in_order(i):
-        crossing = jnp.where(jnp.logical_or(i == 2, i >= 5), 1, 0)
-        before = jnp.where(i >= 5, i - 4, jnp.where(i == 2, 0, jnp.where(i > 2, i - 1, i)))
-        return crossing, before
+    def group_at(k, turned_by):
+        part = (high_part + k // ys) % 2
+        return part * ys + (my_y + ys - (k + turned_by) % ys) % ys
 
     def round_one(k):
-        group = group_of(*in_order(k))
+        group = group_at(k, 0)
         span = pl.ds(group * group_modes, group_modes)
         wait_group(blocks, a2a_recv, group)
         turned = turn(0, blocks[span].reshape(group_rows, width))
         first[span] = turned[:, :half].reshape(group_modes, delays, half)
         second[span] = turned[:, half:].reshape(group_modes, delays, half)
-        crossing, step = in_order(k)
-
-        @pl.when(jnp.logical_or(jnp.logical_not(is_last), jnp.logical_and(hands_over, crossing + step == 0)))
+
+        @pl.when(jnp.logical_not(is_last))
         def _():
             send_next(group).start()
 
-        @pl.when(jnp.logical_and(hands_over, jnp.logical_and(crossing == 0, step > 0)))
-        def _():
-            to_relay(group, step).start()
-
         add_gram(0, turned)
 
-    wraps = jnp.logical_and(my_place == 0, me != run)
+    wraps = jnp.where(jnp.logical_and(my_place == 0, jnp.logical_not(is_head)), 1, 0)
 
     def round_two(k):
         @pl.when(jnp.logical_and(is_head, k == 0))
@@ -292,17 +300,14 @@
             before_high[...] = high
             before_low[...] = low
 
-        crossing, step = in_order(k)
-        group = jnp.where(wraps, group_of(k // ys, k % ys + 1), group_of(crossing, step))
+        group = group_at(k, wraps)
         span = pl.ds(group * group_modes, group_modes)
 
-        raw = jnp.logical_and(is_head, jnp.logical_or(in_high, group // ys == 0))
-
-        @pl.when(jnp.logical_not(raw))
+        @pl.when(jnp.logical_not(is_head))
         def _():
             send_next(group).wait_recv()
 
-        @pl.when(raw)
+        @pl.when(is_head)
         def _():
             wait_group(extra, extra_recv, group)
             high, low = split(extra[span].reshape(group_rows, width))
@@ -345,43 +350,36 @@
         pltpu.make_async_copy(gram_ref.at[r], gram_out.at[r], gram_sem.at[r]).start()
 
     round_one(0)
-    round_one(1)
-
-    @pl.loop(2, GROUPS)
+
+    @pl.loop(1, GROUPS)
     def _(k):
-        pass_on(k)
         round_one(k)
-        round_two(k - 2)
+        round_two(k - 1)
+
+    @pl.when(in_high)
+    def _():
+        pl.semaphore_wait(rows_all_in, 1)
 
     finish(0)
-    round_two(GROUPS - 2)
     round_two(GROUPS - 1)
     finish(1)
     collect(0)
     everything = stage.at[pl.ds(0, snaps - 1)]
     pltpu.make_async_copy(everything, everything, a2a_send).wait()
-    one = extra_stage.at[0]
-
-    @pl.when(jnp.logical_and(in_low, me > 0))
-    def _():
-        pltpu.make_async_copy(extra_stage, extra_stage, extra_send).wait()
-
-    @pl.when(jnp.logical_or(me == 0, me > run))
+    two = stage.at[pl.ds(0, 2)]
+    one = stage.at[0]
+
+    @pl.when(is_head)
     def _():
         pltpu.make_async_copy(one, one, extra_send).wait()
 
-    @pl.when(is_relay)
-    def _():
-        relay_out.wait_send()
+    @pl.when(jnp.logical_not(is_head))
+    def _():
+        pltpu.make_async_copy(two, two, extra_send).wait()
 
     @pl.when(is_last)
     def _():
         before_copy.wait_send()
-
-    @pl.when(hands_over)
-    def _():
-        sent = second.at[pl.ds(0, run * modes)]
-        pltpu.make_async_copy(sent, sent, next_send).wait()
 
     @pl.when(jnp.logical_not(is_last))
     def _():
@@ -442,7 +440,6 @@
             pltpu.VMEM((snaps * modes, delays, half), f32),
             pltpu.VMEM((snaps * modes, delays, half), f32),
             pltpu.VMEM((snaps * modes, delays, half), f32),
-            pltpu.VMEM((snaps // GROUPS * modes, delays, half), f32),
             pltpu.VMEM((snaps * modes, delays, width), f32),
             pltpu.VMEM((2, width, width), bf16),
             pltpu.VMEM((2, width, width), bf16),
@@ -462,11 +459,13 @@
             pltpu.SemaphoreType.DMA,
             pltpu.SemaphoreType.DMA((GROUPS,)),
             pltpu.SemaphoreType.DMA,
-            pltpu.SemaphoreType.DMA,
-            pltpu.SemaphoreType.DMA,
             pltpu.SemaphoreType.DMA((2,)),
             pltpu.SemaphoreType.DMA((2, rows)),
             pltpu.SemaphoreType.DMA((2, rows)),
+            pltpu.SemaphoreType.REGULAR,
+            pltpu.SemaphoreType.REGULAR,
+            pltpu.SemaphoreType.REGULAR,
+            pltpu.SemaphoreType.REGULAR,
         ],
         compiler_params=pltpu.CompilerParams(
             collective_id=0, has_side_effects=True, vmem_limit_bytes=60 * 1024 * 1024

time: 55.8 us -> 60.6 us (1.086)
  the two profiles are of different devices: /device:TPU:32 before, /device:TPU:226 now
where the time goes in v4:
time: 60.6 us; the launch traced here: 60.5 us
  Pallas kernels  59.9 us (99%)
  between operations  0.64 us (1%)
    pallas_call x1, Pallas kernels, body(): pl.pallas_call(functools.partial(kernel, sizes), out_shape=out_shape, in_...  57.7 us
    pallas_call x1, Pallas kernels, body(): pl.pallas_call(write_results, out_shape=out_shape, in_specs=[hbm, hbm], o...  2.15 us

profile of v4, /device:TPU:226, one launch (start us, length us, event | category | flops | bytes accessed | tf_op | source)
XLA Modules:
  0.0 60.5 jit_solution(10906124463244448197)
XLA Ops:
  0.6 57.7 %rounds.1 = (f32[128,8,256]{2,1,0:T(8,128)}, f32[2,1,64,256]{3,2,1,0:T(8,128)}) custom-call(s32[128]{0:T(128)} %order_hbm.1, f32[2,128,8,128]{3,2,1,0:T(8,128)} %bitcast.3, f32[2,1,256,256]{3,2,1,0:T(8,128)} %rot_hbm.1), custom_call_target="tpu_custom_call" | custom-call | tf_op jit(solution)/shard_map/rounds/pallas_call | solution.py:426
  58.4 2.1 %write_results.1 = (f32[128,8,256]{2,1,0:T(8,128)}, f32[2,1,64,256]{3,2,1,0:T(8,128)}) custom-call(f32[128,8,256]{2,1,0:T(8,128)} %get-tuple-element.4.out_from, f32[2,1,64,256]{3,2,1,0:T(8,128)} %get-tuple-element.5.gram_from), custom_call_target="tpu_custom_call" | custom-call | tf_op jit(solution)/shard_map/write_results/pallas_call | solution.py:475

commit v5 on v2

v5 whole, which is shorter than its diff:
```python
import functools

import jax
import jax.numpy as jnp
from jax import lax
from jax.experimental import pallas as pl
from jax.experimental.pallas import tpu as pltpu
from jax.sharding import PartitionSpec as P

MESH = pl.DeviceIdType.MESH
BATCH = 4
EARLY = 8
HELPER = 3
GROUPS = 8


def split(value):
    high = value.astype(jnp.bfloat16)
    low = (value - high.astype(jnp.float32)).astype(jnp.bfloat16)
    return high, low


def dot(left, right):
    return jnp.dot(left, right, preferred_element_type=jnp.float32)


def dot_rows(left, right):
    return lax.dot_general(left, right, (((0,), (0,)), ((), ())), preferred_element_type=jnp.float32)


def kernel(
    sizes,
    order_hbm,
    x_hbm,
    rot_hbm,
    out_ref,
    gram_ref,
    order_ref,
    x_ref,
    rot_ref,
    rot_before,
    stage,
    over,
    landed,
    rot_landed,
    blocks,
    extra,
    helped,
    first,
    second,
    arrived,
    rot_high,
    rot_low,
    before_high,
    before_low,
    shares,
    share_in,
    load_sem,
    a2a_send,
    a2a_recv,
    extra_send,
    extra_recv,
    before_send,
    before_recv,
    over_send,
    over_recv,
    rot_send,
    rot_recv,
    help_send,
    partner_in,
    partners_in,
    half_in,
    rows_in,
    rows_all_in,
    next_send,
    next_recv,
    share_send,
    share_recv,
):
    snaps, rows, modes, delays, width = sizes
    half = width // 2
    per_group = snaps // GROUPS
    group_modes = modes * per_group
    group_rows = group_modes * delays
    share_rows = width // rows
    scale = 1.0 / float(modes * snaps * delays * rows)

    me = lax.axis_index("snap")
    row = lax.axis_index("row")
    my_group = me // per_group
    after = (me + 1) % snaps
    run = snaps // 2
    is_head = me % run == 0
    is_last = me % run == run - 1

    loads = [
        pltpu.make_async_copy(order_hbm, order_ref, load_sem.at[0]),
        pltpu.make_async_copy(x_hbm, x_ref, load_sem.at[1]),
        pltpu.make_async_copy(rot_hbm, rot_ref, load_sem.at[2]),
    ]
    for load in loads:
        load.start()

    barrier = pltpu.get_barrier_semaphore()
    high_part = me // run
    in_low, in_high = high_part == 0, high_part == 1
    my_head = high_part * run
    across = (me + run) % snaps
    my_span = pl.ds(me * modes, modes)
    across_span = pl.ds(across * modes, modes)
    across_group = across // per_group
    ys = GROUPS // 2
    my_y = my_group % ys
    my_place = me % per_group

    def signal(semaphore, snap, to_row):
        pl.semaphore_signal(
            semaphore, inc=1, device_id={"snap": snap, "row": to_row}, device_id_type=MESH
        )

    def remote(source, target, send, recv, snap):
        return pltpu.make_async_remote_copy(
            src_ref=source,
            dst_ref=target,
            send_sem=send,
            recv_sem=recv,
            device_id={"snap": snap, "row": row},
            device_id_type=MESH,
        )

    def place_at(i):
        k, j = i // per_group, i % per_group
        return ((my_y + k) % ys) * per_group + (my_place + j) % per_group

    def take(target, d):
        target[:, :, :half] = x_ref[:, order_ref[2 * d]]
        target[:, :, half:] = x_ref[:, order_ref[2 * d + 1]]

    def cross_copy(batch):
        span = pl.ds(batch * BATCH, BATCH)
        return remote(over.at[span], landed.at[span], over_send, over_recv.at[batch], across)

    def cross_extra():
        return remote(over.at[EARLY], landed.at[EARLY], over_send, over_recv.at[batches], across)

    def send_across():
        @pl.when(is_last)
        def _():
            rot_across.start()

        @pl.loop(0, batches)
        def _(batch):
            @pl.loop(0, BATCH)
            def _(j):
                i = batch * BATCH + j
                take(over.at[i], (run - my_head) + place_at(i))

            cross_copy(batch).start()

            @pl.when(batch == 1)
            def _():
                take(over.at[EARLY], (run - my_head + snaps - 1) % snaps)
                cross_extra().start()

    helper = my_head + my_y * per_group + HELPER
    is_helper = my_place == HELPER
    place_span = pl.ds(my_place * modes, modes)
    other_pair = (my_head + snaps - 1) % snaps

    def send_inside(i):
        d = my_head + place_at(i)
        take(stage.at[i], d)
        remote(stage.at[i], blocks.at[my_span], a2a_send, a2a_recv.at[my_group], d).start()

        @pl.when(d == helper)
        def _():
            take(stage.at[0], other_pair)
            remote(
                stage.at[0], extra.at[0, place_span], extra_send, extra_recv.at[0], helper
            ).start()

    def send_direct(i):
        d = run - my_head + place_at(i)
        take(stage.at[run + i], d)
        remote(stage.at[run + i], blocks.at[my_span], a2a_send, a2a_recv.at[my_group], d).start()

    batches = EARLY // BATCH
    rot_across = remote(
        rot_ref.at[0, 0, :, pl.ds(half, half)], rot_landed, before_send, rot_recv, across
    )
    rot_on = [
        remote(rot_landed, rot_before, rot_send.at[y], before_recv, my_head + y * per_group + HELPER)
        for y in range(ys)
    ]

    def prepare():
        take(blocks.at[my_span], me)

        @pl.when(is_helper)
        def _():
            take(extra.at[0, place_span], other_pair)

        for r in range(2):
            high, low = split(rot_ref[r, 0])
            rot_high[r] = high
            rot_low[r] = low
        shares[...] = jnp.zeros_like(shares)

    @pl.when(in_low)
    def _():
        signal(barrier, across, row)

        @pl.loop(1, run)
        def _(i):
            signal(barrier, (me + i) % run, row)

        for i in range(1, rows):
            signal(barrier, me, (row + i) % rows)

        for load in loads:
            load.wait()
        pl.semaphore_wait(barrier, run - 1 + rows - 1)
        pl.semaphore_wait(partner_in, 1)

        @pl.loop(1, run)
        def _(i):
            signal(partners_in, (me + i) % run, row)

        send_across()

        @pl.loop(1, run)
        def _(i):
            send_inside(i)

        pl.semaphore_wait(partners_in, run - 1)
        signal(half_in, across, row)
        for i in range(1, rows):
            signal(rows_in, me, (row + i) % rows)

        @pl.loop(EARLY, run)
        def _(i):
            send_direct(i)

        prepare()
        pl.semaphore_wait(rows_in, rows - 1)
        signal(rows_all_in, across, row)

    @pl.when(in_high)
    def _():
        pl.semaphore_wait(barrier, 1)
        signal(partner_in, across, row)
        for load in loads:
            load.wait()
        send_across()
        prepare()
        pl.semaphore_wait(half_in, 1)

        @pl.loop(1, run)
        def _(i):
            @pl.when(i >= EARLY)
            def _():
                send_direct(i)

            send_inside(i)


    def pass_on(batch):
        cross_copy(batch).wait_recv()

        @pl.loop(0, BATCH)
        def _(j):
            i = batch * BATCH + j
            d = my_head + place_at(i)

            @pl.when(i == 0)
            def _():
                blocks[across_span] = landed[0]

            @pl.when(i > 0)
            def _():
                remote(
                    landed.at[i], blocks.at[across_span], a2a_send, a2a_recv.at[across_group], d
                ).start()

    def pass_extra_on():
        cross_extra().wait_recv()

        @pl.when(is_helper)
        def _():
            extra[1, place_span] = landed[EARLY]

        @pl.when(jnp.logical_not(is_helper))
        def _():
            remote(
                landed.at[EARLY], extra.at[1, place_span], extra_send, extra_recv.at[1], helper
            ).start()

    def help_first(side):
        group = (my_group, across_group)[side]
        part = extra.at[side, pl.ds(0, group_modes - modes)]
        pltpu.make_async_copy(part, part, extra_recv.at[side]).wait()
        high, low = split(extra[side].reshape(group_rows, width))
        other = dot(high, before_high[...]) + (
            dot(high, before_low[...]) + dot(low, before_high[...])
        )
        helped[side] = other.reshape(group_modes, delays, half)
        help_copy(side, group).start()

    def help_copy(side, group):
        span = pl.ds(group * group_modes, group_modes)
        return remote(
            helped.at[side], arrived.at[span], help_send.at[side], next_recv.at[group], my_head
        )

    def pass_on_all():
        @pl.when(is_last)
        def _():
            rot_across.wait_recv()
            for copy in rot_on:
                copy.start()

        for batch in range(batches):
            pass_on(batch)
        pass_extra_on()

    def wait_group(buffer, sems, group):
        whole = buffer.at[pl.ds(0, group_modes)]
        part = buffer.at[pl.ds(0, group_modes - modes)]

        @pl.when(group % ys == my_y)
        def _():
            pltpu.make_async_copy(part, part, sems.at[group]).wait()

        @pl.when(group % ys != my_y)
        def _():
            pltpu.make_async_copy(whole, whole, sems.at[group]).wait()

    def turn(r, matrix):
        high, low = split(matrix)
        return dot(high, rot_high[r]) + (dot(high, rot_low[r]) + dot(low, rot_high[r]))

    def add_gram(r, turned):
        high, low = split(turned)
        part = dot_rows(high, high) + (dot_rows(high, low) + dot_rows(low, high))
        shares[r] += part.reshape(rows, share_rows, width)

    def send_next(group):
        span = pl.ds(group * group_modes, group_modes)
        return pltpu.make_async_remote_copy(
            src_ref=second.at[span],
            dst_ref=arrived.at[span],
            send_sem=next_send,
            recv_sem=next_recv.at[group],
            device_id={"snap": after, "row": row},
            device_id_type=MESH,
        )

    def group_of(crossing, k):
        return (high_part + crossing) % 2 * ys + (my_y + ys - k % ys) % ys

    def in_order(i):
        crossing = jnp.where(jnp.logical_or(i == 2, i >= 5), 1, 0)
        before = jnp.where(i >= 5, i - 4, jnp.where(i == 2, 0, jnp.where(i > 2, i - 1, i)))
        return crossing, before

    def round_one(k):
        group = group_of(*in_order(k))
        span = pl.ds(group * group_modes, group_modes)
        wait_group(blocks, a2a_recv, group)
        turned = turn(0, blocks[span].reshape(group_rows, width))
        first[span] = turned[:, :half].reshape(group_modes, delays, half)
        second[span] = turned[:, half:].reshape(group_modes, delays, half)

        @pl.when(jnp.logical_not(is_last))
        def _():
            send_next(group).start()

        add_gram(0, turned)

    wraps = jnp.logical_and(my_place == 0, jnp.logical_not(is_head))

    def round_two(k):
        crossing, step = in_order(k)
        group = jnp.where(wraps, group_of(k // ys, k % ys + 1), group_of(crossing, step))
        span = pl.ds(group * group_modes, group_modes)

        send_next(group).wait_recv()
        matrix = jnp.concatenate([first[span], arrived[span]], axis=2)
        turned = turn(1, matrix.reshape(group_rows, width))
        out_ref[span] = turned.reshape(group_modes, delays, width)
        add_gram(1, turned)

    def finish(r):
        for i in range(1, rows):
            share_copy(r, i).start()

    def share_copy(r, i):
        to = (row + i) % rows
        return pltpu.make_async_remote_copy(
            src_ref=shares.at[r, to],
            dst_ref=share_in.at[r, i],
            send_sem=share_send.at[r, i],
            recv_sem=share_recv.at[r, i],
            device_id={"snap": me, "row": to},
            device_id_type=MESH,
        )

    def collect(r):
        for i in range(1, rows):
            share_copy(r, i).wait()
        total = shares[r, row]
        for i in range(1, rows):
            total = total + share_in[r, i]
        gram_ref[r, 0] = total * scale

    pass_on_all()

    @pl.loop(0, GROUPS)
    def _(k):
        round_one(k)

        @pl.when(jnp.logical_and(is_helper, k == 3))
        def _():
            rot_on[0].wait_recv()
            high, low = split(rot_before[...])
            before_high[...] = high
            before_low[...] = low
            for side in range(2):
                help_first(side)

        @pl.loop(jnp.where(k == 6, 4, 0), jnp.where(k == 5, 4, jnp.where(k == 6, 6, 0)))
        def _(j):
            round_two(j)

    @pl.when(in_high)
    def _():
        pl.semaphore_wait(rows_all_in, 1)

    finish(0)

    @pl.loop(GROUPS - 2, GROUPS)
    def _(j):
        round_two(j)

    finish(1)
    collect(0)
    sent = blocks.at[pl.ds(0, 2 * (run - 1) * modes)]
    pltpu.make_async_copy(sent, sent, a2a_send).wait()
    pltpu.make_async_copy(over, over, over_send).wait()

    @pl.when(jnp.logical_not(is_helper))
    def _():
        two = stage.at[pl.ds(0, 2)]
        pltpu.make_async_copy(two, two, extra_send).wait()

    @pl.when(is_helper)
    def _():
        for side in range(2):
            help_copy(side, (my_group, across_group)[side]).wait_send()

    @pl.when(is_last)
    def _():
        rot_across.wait_send()
        for copy in rot_on:
            copy.wait_send()

    @pl.when(jnp.logical_not(is_last))
    def _():
        pltpu.make_async_copy(second, second, next_send).wait()

    collect(1)


def write_results(out_from, gram_from, out_ref, gram_ref, sems):
    copies = [
        pltpu.make_async_copy(out_from, out_ref, sems.at[0]),
        pltpu.make_async_copy(gram_from, gram_ref, sems.at[1]),
    ]
    for copy in copies:
        copy.start()
    for copy in copies:
        copy.wait()


def body(delay_matrix, arrangement, rotations):
    modes, delays, columns = delay_matrix.shape
    snaps = lax.axis_size("snap")
    rows = lax.axis_size("row")
    width = columns // snaps
    half = width // 2
    share_rows = width // rows
    sizes = (snaps, rows, modes, delays, width)
    f32, bf16 = jnp.float32, jnp.bfloat16
    blocks = delay_matrix.reshape(modes, delays, 2 * snaps, half).transpose(0, 2, 1, 3)
    hbm = pl.BlockSpec(memory_space=pltpu.HBM)
    vmem = pl.BlockSpec(memory_space=pltpu.VMEM)
    out_shape = (
        jax.ShapeDtypeStruct((snaps * modes, delays, width), f32),
        jax.ShapeDtypeStruct((2, 1, share_rows, width), f32),
    )
    rotated, grams = pl.pallas_call(
        functools.partial(kernel, sizes),
        out_shape=tuple(pltpu.VMEM(s.shape, s.dtype) for s in out_shape),
        in_specs=[hbm, hbm, hbm],
        out_specs=(vmem, vmem),
        scratch_shapes=[
            pltpu.SMEM(arrangement.shape, arrangement.dtype),
            pltpu.VMEM(blocks.shape, f32),
            pltpu.VMEM(rotations.shape, f32),
            pltpu.VMEM((width, half), f32),
            pltpu.VMEM((snaps, modes, delays, width), f32),
            pltpu.VMEM((EARLY + 1, modes, delays, width), f32),
            pltpu.VMEM((EARLY + 1, modes, delays, width), f32),
            pltpu.VMEM((width, half), f32),
            pltpu.VMEM((snaps * modes, delays, width), f32),
            pltpu.VMEM((2, snaps // GROUPS * modes, delays, width), f32),
            pltpu.VMEM((2, snaps // GROUPS * modes, delays, half), f32),
            pltpu.VMEM((snaps * modes, delays, half), f32),
            pltpu.VMEM((snaps * modes, delays, half), f32),
            pltpu.VMEM((snaps * modes, delays, half), f32),
            pltpu.VMEM((2, width, width), bf16),
            pltpu.VMEM((2, width, width), bf16),
            pltpu.VMEM((width, half), bf16),
            pltpu.VMEM((width, half), bf16),
            pltpu.VMEM((2, rows, share_rows, width), f32),
            pltpu.VMEM((2, rows, share_rows, width), f32),
            pltpu.SemaphoreType.DMA((3,)),
            pltpu.SemaphoreType.DMA,
            pltpu.SemaphoreType.DMA((GROUPS,)),
            pltpu.SemaphoreType.DMA,
            pltpu.SemaphoreType.DMA((2,)),
            pltpu.SemaphoreType.DMA,
            pltpu.SemaphoreType.DMA,
            pltpu.SemaphoreType.DMA,
            pltpu.SemaphoreType.DMA((EARLY // BATCH + 1,)),
            pltpu.SemaphoreType.DMA((GROUPS // 2,)),
            pltpu.SemaphoreType.DMA,
            pltpu.SemaphoreType.DMA((2,)),
            pltpu.SemaphoreType.REGULAR,
            pltpu.SemaphoreType.REGULAR,
            pltpu.SemaphoreType.REGULAR,
            pltpu.SemaphoreType.REGULAR,
            pltpu.SemaphoreType.REGULAR,
            pltpu.SemaphoreType.DMA,
            pltpu.SemaphoreType.DMA((GROUPS,)),
            pltpu.SemaphoreType.DMA((2, rows)),
            pltpu.SemaphoreType.DMA((2, rows)),
        ],
        compiler_params=pltpu.CompilerParams(
            collective_id=0, has_side_effects=True, vmem_limit_bytes=60 * 1024 * 1024
        ),
        name="rounds",
    )(arrangement, blocks, rotations)
    return pl.pallas_call(
        write_results,
        out_shape=out_shape,
        in_specs=[vmem, vmem],
        out_specs=(hbm, hbm),
        scratch_shapes=[pltpu.SemaphoreType.DMA((2,))],
        name="write_results",
    )(
        pltpu.with_memory_space_constraint(rotated, pltpu.VMEM),
        pltpu.with_memory_space_constraint(grams, pltpu.VMEM),
    )


def solution(mesh):
    placed = (P("snap", "row", None), P(), P(None, "snap", None, None))
    return jax.shard_map(
        body,
        mesh=mesh,
        in_specs=placed,
        out_specs=(P(None, "row", "snap"), P(None, "snap", "row", None)),
        check_vma=False,
    )
```

time: 58.6 us -> 53.7 us (0.916)
  the two profiles are of different devices: /device:TPU:1 before, /device:TPU:224 now
where the time goes in v5:
time: 53.7 us; the launch traced here: 53.6 us
  Pallas kernels  52.9 us (99%)
  between operations  0.64 us (1%)
    pallas_call x1, Pallas kernels, body(): pl.pallas_call(functools.partial(kernel, sizes), out_shape=tuple((pltpu.V...  51.9 us

profile of v5, /device:TPU:224, one launch (start us, length us, event | category | flops | bytes accessed | tf_op | source)
XLA Modules:
  0.0 53.6 jit_solution(3603747511155889338)
XLA Ops:
  0.6 51.9 %rounds.1 = (f32[128,8,256]{2,1,0:T(8,128)S(1)}, f32[2,1,64,256]{3,2,1,0:T(8,128)S(1)}) custom-call(s32[128]{0:T(128)} %order_hbm.1, f32[2,128,8,128]{3,2,1,0:T(8,128)} %bitcast.3, f32[2,1,256,256]{3,2,1,0:T(8,128)} %rot_hbm.1), custom_call_target="tpu_custom_call" | custom-call | tf_op jit(solution)/shard_map/rounds/pallas_call | solution.py:501
  52.5 1.0 %write_results.1 = (f32[128,8,256]{2,1,0:T(8,128)}, f32[2,1,64,256]{3,2,1,0:T(8,128)}) custom-call(f32[128,8,256]{2,1,0:T(8,128)S(1)} %get-tuple-element.4.out_from, f32[2,1,64,256]{3,2,1,0:T(8,128)S(1)} %get-tuple-element.5.gram_from), custom_call_target="tpu_custom_call" | custom-call | tf_op jit(solution)/shard_map/write_results/pallas_call | solution.py:554

commit v6 on v5

--- a/solution.py
+++ b/solution.py
@@ -220,6 +220,7 @@
         for load in loads:
             load.wait()
         pl.semaphore_wait(barrier, run - 1 + rows - 1)
+        signal(barrier, across, row)
         pl.semaphore_wait(partner_in, 1)
 
         @pl.loop(1, run)
@@ -252,15 +253,17 @@
         for load in loads:
             load.wait()
         send_across()
+        pl.semaphore_wait(barrier, 1)
+
+        @pl.loop(EARLY, run)
+        def _(i):
+            send_direct(i)
+
         prepare()
         pl.semaphore_wait(half_in, 1)
 
         @pl.loop(1, run)
         def _(i):
-            @pl.when(i >= EARLY)
-            def _():
-                send_direct(i)
-
             send_inside(i)
 
 

time: 53.7 us -> 52.4 us (0.976)
  Pallas kernels: 52.9 us -> 51.3 us
    pallas_call x1, Pallas kernels: 51.9 us -> 50.3 us  [body(): pl.pallas_call(functools.partial(kernel, sizes), out_shape=tuple((pltpu.V...]
where the time goes in v6:
time: 52.4 us; the launch traced here: 52 us
  Pallas kernels  51.3 us (98%)
  between operations  0.64 us (1%)
    pallas_call x1, Pallas kernels, body(): pl.pallas_call(functools.partial(kernel, sizes), out_shape=tuple((pltpu.V...  50.3 us

profile of v6, /device:TPU:224, one launch (start us, length us, event | category | flops | bytes accessed | tf_op | source)
XLA Modules:
  0.0 52.0 jit_solution(6413399683830886171)
XLA Ops:
  0.6 50.3 %rounds.1 = (f32[128,8,256]{2,1,0:T(8,128)S(1)}, f32[2,1,64,256]{3,2,1,0:T(8,128)S(1)}) custom-call(s32[128]{0:T(128)} %order_hbm.1, f32[2,128,8,128]{3,2,1,0:T(8,128)} %bitcast.3, f32[2,1,256,256]{3,2,1,0:T(8,128)} %rot_hbm.1), custom_call_target="tpu_custom_call" | custom-call | tf_op jit(solution)/shard_map/rounds/pallas_call | solution.py:504
  51.0 1.0 %write_results.1 = (f32[128,8,256]{2,1,0:T(8,128)}, f32[2,1,64,256]{3,2,1,0:T(8,128)}) custom-call(f32[128,8,256]{2,1,0:T(8,128)S(1)} %get-tuple-element.4.out_from, f32[2,1,64,256]{3,2,1,0:T(8,128)S(1)} %get-tuple-element.5.gram_from), custom_call_target="tpu_custom_call" | custom-call | tf_op jit(solution)/shard_map/write_results/pallas_call | solution.py:557

commit v7 on v6

--- a/solution.py
+++ b/solution.py
@@ -10,7 +10,7 @@
 MESH = pl.DeviceIdType.MESH
 BATCH = 4
 EARLY = 8
-HELPER = 3
+HELPER = 6
 GROUPS = 8
 
 
@@ -385,6 +385,7 @@
     def round_two(k):
         crossing, step = in_order(k)
         group = jnp.where(wraps, group_of(k // ys, k % ys + 1), group_of(crossing, step))
+        group = jnp.where(is_head, group_of(k // ys, k % ys), group)
         span = pl.ds(group * group_modes, group_modes)
 
         send_next(group).wait_recv()
@@ -428,8 +429,11 @@
             high, low = split(rot_before[...])
             before_high[...] = high
             before_low[...] = low
-            for side in range(2):
-                help_first(side)
+            help_first(0)
+
+        @pl.when(jnp.logical_and(is_helper, k == 5))
+        def _():
+            help_first(1)
 
         @pl.loop(jnp.where(k == 6, 4, 0), jnp.where(k == 5, 4, jnp.where(k == 6, 6, 0)))
         def _(j):

time: 52.4 us -> 50.9 us (0.971)
  the two profiles are of different devices: /device:TPU:224 before, /device:TPU:160 now
where the time goes in v7:
time: 50.9 us; the launch traced here: 50.8 us
  Pallas kernels  50.2 us (99%)
  between operations  0.64 us (1%)
    pallas_call x1, Pallas kernels, body(): pl.pallas_call(functools.partial(kernel, sizes), out_shape=tuple((pltpu.V...  49.1 us
    pallas_call x1, Pallas kernels, body(): pl.pallas_call(write_results, out_shape=out_shape, in_specs=[vmem, vmem],...  1.02 us

profile of v7, /device:TPU:160, one launch (start us, length us, event | category | flops | bytes accessed | tf_op | source)
XLA Modules:
  0.0 50.8 jit_solution(9299606006409234747)
XLA Ops:
  0.6 49.1 %rounds.1 = (f32[128,8,256]{2,1,0:T(8,128)S(1)}, f32[2,1,64,256]{3,2,1,0:T(8,128)S(1)}) custom-call(s32[128]{0:T(128)} %order_hbm.1, f32[2,128,8,128]{3,2,1,0:T(8,128)} %bitcast.3, f32[2,1,256,256]{3,2,1,0:T(8,128)} %rot_hbm.1), custom_call_target="tpu_custom_call" | custom-call | tf_op jit(solution)/shard_map/rounds/pallas_call | solution.py:508
  49.8 1.0 %write_results.1 = (f32[128,8,256]{2,1,0:T(8,128)}, f32[2,1,64,256]{3,2,1,0:T(8,128)}) custom-call(f32[128,8,256]{2,1,0:T(8,128)S(1)} %get-tuple-element.4.out_from, f32[2,1,64,256]{3,2,1,0:T(8,128)S(1)} %get-tuple-element.5.gram_from), custom_call_target="tpu_custom_call" | custom-call | tf_op jit(solution)/shard_map/write_results/pallas_call | solution.py:561

commit v8 on v7

--- a/solution.py
+++ b/solution.py
@@ -55,6 +55,7 @@
     before_low,
     shares,
     share_in,
+    merge_in,
     load_sem,
     a2a_send,
     a2a_recv,
@@ -76,6 +77,8 @@
     next_recv,
     share_send,
     share_recv,
+    merge_send,
+    merge_recv,
 ):
     snaps, rows, modes, delays, width = sizes
     half = width // 2
@@ -394,28 +397,74 @@
         out_ref[span] = turned.reshape(group_modes, delays, width)
         add_gram(1, turned)
 
-    def finish(r):
-        for i in range(1, rows):
-            share_copy(r, i).start()
+    inner = jnp.logical_or(row == 1, row == 2)
+    outer = jnp.logical_not(inner)
+    near = row + 1 - 2 * (row % 2)
+
+    def row_copy(source, target, send, recv, to):
+        return pltpu.make_async_remote_copy(
+            src_ref=source,
+            dst_ref=target,
+            send_sem=send,
+            recv_sem=recv,
+            device_id={"snap": me, "row": to},
+            device_id_type=MESH,
+        )
 
     def share_copy(r, i):
         to = (row + i) % rows
-        return pltpu.make_async_remote_copy(
-            src_ref=shares.at[r, to],
-            dst_ref=share_in.at[r, i],
-            send_sem=share_send.at[r, i],
-            recv_sem=share_recv.at[r, i],
-            device_id={"snap": me, "row": to},
-            device_id_type=MESH,
-        )
+        return row_copy(
+            shares.at[r, to], share_in.at[r, i], share_send.at[r, i], share_recv.at[r, i], to
+        )
+
+    def merge_copy(r):
+        return row_copy(
+            shares.at[r, rows - 1 - row], merge_in.at[r], merge_send.at[r], merge_recv.at[r], near
+        )
+
+    def skips(i):
+        return jnp.logical_and(outer, (row + i) % rows == rows - 1 - row)
+
+    def finish(r):
+        @pl.when(outer)
+        def _():
+            merge_copy(r).start()
+
+        for i in range(1, rows):
+
+            @pl.when(jnp.logical_not(jnp.logical_or(skips(i), jnp.logical_and(inner, i == 2))))
+            def _():
+                share_copy(r, i).start()
+
+    def forward(r):
+        @pl.when(inner)
+        def _():
+            merge_copy(r).wait_recv()
+            far = (row + 2) % rows
+            shares[r, far] = shares[r, far] + merge_in[r]
+            share_copy(r, 2).start()
 
     def collect(r):
+        total = shares[r, row]
+        gram_ref[r, 0] = total
+
         for i in range(1, rows):
-            share_copy(r, i).wait()
-        total = shares[r, row]
-        for i in range(1, rows):
-            total = total + share_in[r, i]
-        gram_ref[r, 0] = total * scale
+            from_far = jnp.logical_and(outer, (row + rows - i) % rows == rows - 1 - row)
+
+            @pl.when(jnp.logical_not(from_far))
+            def _():
+                share_copy(r, i).wait_recv()
+                gram_ref[r, 0] += share_in[r, i]
+
+            @pl.when(jnp.logical_not(skips(i)))
+            def _():
+                share_copy(r, i).wait_send()
+
+        gram_ref[r, 0] = gram_ref[r, 0] * scale
+
+        @pl.when(outer)
+        def _():
+            merge_copy(r).wait_send()
 
     pass_on_all()
 
@@ -435,7 +484,9 @@
         def _():
             help_first(1)
 
-        @pl.loop(jnp.where(k == 6, 4, 0), jnp.where(k == 5, 4, jnp.where(k == 6, 6, 0)))
+        early = jnp.where(is_head, 0, 4)
+
+        @pl.loop(jnp.where(k == 6, early, 0), jnp.where(k == 5, early, jnp.where(k == 6, 6, 0)))
         def _(j):
             round_two(j)
 
@@ -449,7 +500,18 @@
     def _(j):
         round_two(j)
 
+    forward(0)
+
+    @pl.when(row == 2)
+    def _():
+        forward(1)
+
     finish(1)
+
+    @pl.when(row == 1)
+    def _():
+        forward(1)
+
     collect(0)
     sent = blocks.at[pl.ds(0, 2 * (run - 1) * modes)]
     pltpu.make_async_copy(sent, sent, a2a_send).wait()
@@ -531,6 +593,7 @@
             pltpu.VMEM((width, half), bf16),
             pltpu.VMEM((2, rows, share_rows, width), f32),
             pltpu.VMEM((2, rows, share_rows, width), f32),
+            pltpu.VMEM((2, share_rows, width), f32),
             pltpu.SemaphoreType.DMA((3,)),
             pltpu.SemaphoreType.DMA,
             pltpu.SemaphoreType.DMA((GROUPS,)),
@@ -552,6 +615,8 @@
             pltpu.SemaphoreType.DMA((GROUPS,)),
             pltpu.SemaphoreType.DMA((2, rows)),
             pltpu.SemaphoreType.DMA((2, rows)),
+            pltpu.SemaphoreType.DMA((2,)),
+            pltpu.SemaphoreType.DMA((2,)),
         ],
         compiler_params=pltpu.CompilerParams(
             collective_id=0, has_side_effects=True, vmem_limit_bytes=60 * 1024 * 1024

time: 50.9 us -> 50.5 us (level)
  the two profiles are of different devices: /device:TPU:160 before, /device:TPU:224 now
where the time goes in v8:
time: 50.5 us; the launch traced here: 50.4 us
  Pallas kernels  49.8 us (99%)
  between operations  0.64 us (1%)
    pallas_call x1, Pallas kernels, body(): pl.pallas_call(functools.partial(kernel, sizes), out_shape=tuple((pltpu.V...  48.8 us
    pallas_call x1, Pallas kernels, body(): pl.pallas_call(write_results, out_shape=out_shape, in_specs=[vmem, vmem],...  1.02 us

profile of v8, /device:TPU:224, one launch (start us, length us, event | category | flops | bytes accessed | tf_op | source)
XLA Modules:
  0.0 50.4 jit_solution(18422370852732206033)
XLA Ops:
  0.6 48.8 %rounds.1 = (f32[128,8,256]{2,1,0:T(8,128)S(1)}, f32[2,1,64,256]{3,2,1,0:T(8,128)S(1)}) custom-call(s32[128]{0:T(128)} %order_hbm.1, f32[2,128,8,128]{3,2,1,0:T(8,128)} %bitcast.3, f32[2,1,256,256]{3,2,1,0:T(8,128)} %rot_hbm.1), custom_call_target="tpu_custom_call" | custom-call | tf_op jit(solution)/shard_map/rounds/pallas_call | solution.py:570
  49.4 1.0 %write_results.1 = (f32[128,8,256]{2,1,0:T(8,128)}, f32[2,1,64,256]{3,2,1,0:T(8,128)}) custom-call(f32[128,8,256]{2,1,0:T(8,128)S(1)} %get-tuple-element.4.out_from, f32[2,1,64,256]{3,2,1,0:T(8,128)S(1)} %get-tuple-element.5.gram_from), custom_call_target="tpu_custom_call" | custom-call | tf_op jit(solution)/shard_map/write_results/pallas_call | solution.py:626

commit v9 on v8

--- a/solution.py
+++ b/solution.py
@@ -496,11 +496,17 @@
 
     finish(0)
 
+    @pl.when(in_low)
+    def _():
+        forward(0)
+
     @pl.loop(GROUPS - 2, GROUPS)
     def _(j):
         round_two(j)
 
-    forward(0)
+    @pl.when(in_high)
+    def _():
+        forward(0)
 
     @pl.when(row == 2)
     def _():

time: 50.5 us -> 50.5 us (level)
  no operation moved by 1% of the time
where the time goes in v9:
time: 50.5 us; the launch traced here: 50.4 us
  Pallas kernels  49.8 us (99%)
  between operations  0.64 us (1%)
    pallas_call x1, Pallas kernels, body(): pl.pallas_call(functools.partial(kernel, sizes), out_shape=tuple((pltpu.V...  48.8 us
    pallas_call x1, Pallas kernels, body(): pl.pallas_call(write_results, out_shape=out_shape, in_specs=[vmem, vmem],...  1.02 us

profile of v9, /device:TPU:224, one launch (start us, length us, event | category | flops | bytes accessed | tf_op | source)
XLA Modules:
  0.0 50.4 jit_solution(13825538073624760895)
XLA Ops:
  0.6 48.8 %rounds.1 = (f32[128,8,256]{2,1,0:T(8,128)S(1)}, f32[2,1,64,256]{3,2,1,0:T(8,128)S(1)}) custom-call(s32[128]{0:T(128)} %order_hbm.1, f32[2,128,8,128]{3,2,1,0:T(8,128)} %bitcast.3, f32[2,1,256,256]{3,2,1,0:T(8,128)} %rot_hbm.1), custom_call_target="tpu_custom_call" | custom-call | tf_op jit(solution)/shard_map/rounds/pallas_call | solution.py:576
  49.4 1.0 %write_results.1 = (f32[128,8,256]{2,1,0:T(8,128)}, f32[2,1,64,256]{3,2,1,0:T(8,128)}) custom-call(f32[128,8,256]{2,1,0:T(8,128)S(1)} %get-tuple-element.4.out_from, f32[2,1,64,256]{3,2,1,0:T(8,128)S(1)} %get-tuple-element.5.gram_from), custom_call_target="tpu_custom_call" | custom-call | tf_op jit(solution)/shard_map/write_results/pallas_call | solution.py:632
